TPU v7x, 512 devices: a whole 4x8x8 slice. The times are simulated.
512 devices in a mesh: tile: 16 (over z, core), depth: 32 (over x, y).
Axes of the slice: x: 4, y: 8, z: 8, core: 2. Of those that a mesh axis runs over, the one named last changes fastest.
Arguments:
- density: bfloat16 [512, 512, 1024], P('depth', 'tile'), may hold values from 0.099609375 to 1.5
- materials: int32 [512, 512, 1024], P('depth', 'tile'), may hold values from 0 to 7
- emit_table: float32 [3, 8], replicated, may hold values from 0.001953125 to 0.015625
- absorb_table: float32 [8], replicated, may hold values from 0.0009765625 to 0.0078125
- depth_order: int32 [32], replicated, may hold values from 0 to 31, each once
Outputs:
- colour: float32 [3, 512, 1024], P(None, ('tile', 'depth'))
- opacity: float32 [512, 1024], P(('tile', 'depth'))
Inputs may be any that keep to these rules, and one draw needn't show every extreme that they name: depth_order names every slab once.
All inputs are finite; a program needn't handle non-finite values.
Results may differ from a plain program's by a relative error of at most 0.0013.
Values may be sent and summed in bfloat16 or wider, within the bound.
No kernel may reach another device: no remote copies, remote signals or barrier semaphores. Data moves between devices by JAX's collectives and lax.ppermute only.
A program may use at most 64 MiB of HBM per device.

v0:
```python
import jax
import jax.numpy as jnp
from jax import lax
from jax.sharding import PartitionSpec as P

MAT = 8


def with_halo(shard, sides, width):
    for axis, dim in sides:
        devices, length = (lax.axis_size(axis), shard.shape[dim])
        up = [(i, (i + 1) % devices) for i in range(devices - 1)]
        down = [(j, i) for i, j in up]
        last = lax.slice_in_dim(shard, length - width, length, axis=dim)
        first = lax.slice_in_dim(shard, 0, width, axis=dim)
        before = lax.ppermute(last, axis, up)
        after = lax.ppermute(first, axis, down)
        shard = jnp.concatenate([before, shard, after], axis=dim)
    return shard


def from_behind(block, axis, distance):
    devices = range(lax.axis_size(axis))
    route = [(i - distance, i) for i in devices if i - distance in devices]
    return lax.ppermute(block, axis, route)


def slab_terms(padded_rows, after_layer, mats, emit_table, absorb_table):
    field = padded_rows[:, 1:-1]
    after = jnp.concatenate([field[1:], after_layer[None]], 0)
    samples = 0.5 * (field + after)
    grad_rows = 0.5 * (padded_rows[:, 2:] - padded_rows[:, :-2])
    padded_cols = jnp.pad(field, ((0, 0), (0, 0), (1, 1)))
    grad_cols = 0.5 * (padded_cols[:, :, 2:] - padded_cols[:, :, :-2])
    shade = 0.6 + 0.4 * jnp.tanh(2.0 * (grad_rows + grad_cols))
    absorb = jnp.zeros_like(field)
    colours = [jnp.zeros_like(field) for channel in range(3)]
    for material in range(MAT):
        hit = mats == material
        absorb = absorb + jnp.where(hit, absorb_table[material], jnp.float32(0.0))
        colours = [
            colours[channel] + jnp.where(hit, emit_table[channel, material], jnp.float32(0.0))
            for channel in range(3)
        ]
    thick = absorb * samples * samples
    inside = jnp.cumsum(thick, 0) - thick
    weight = samples * shade * jnp.exp(-inside)
    image = jnp.stack([jnp.sum(colours[channel] * weight, 0) for channel in range(3)], axis=1)
    return (image, jnp.sum(thick, 0))


def shards(density, materials, emit_table, absorb_table, depth_order):
    padded = with_halo(density, (("tile", 1),), 1).astype(jnp.float32)
    after_layer = from_behind(density[0], "depth", -1).astype(jnp.float32)
    image, thick = slab_terms(padded, after_layer, materials, emit_table, absorb_table)
    slabs = lax.axis_size("depth")
    mine = lax.axis_index("depth")
    positions = jnp.arange(slabs, dtype=jnp.int32)
    rank_table = jnp.sum(
        jnp.where(depth_order[None, :] == positions[:, None], positions[None, :], 0), axis=1
    )
    my_rank = lax.dynamic_index_in_dim(rank_table, mine, 0, keepdims=False)
    ahead = (rank_table < my_rank).astype(jnp.float32)
    front = jnp.zeros_like(thick) + jnp.sum(
        lax.all_gather(thick[None].astype(jnp.bfloat16), "depth", axis=0, tiled=True).astype(
            jnp.float32
        )
        * ahead[:, None, None],
        0,
    )
    terms = jnp.concatenate([image * jnp.exp(-front)[:, None, :], thick[:, None, :]], 1)
    totals = lax.psum_scatter(terms, "depth", scatter_dimension=0, tiled=True)
    colour = totals[:, :3]
    opacity = 1.0 - jnp.exp(-totals[:, 3])
    return (jnp.transpose(colour, (1, 0, 2)), opacity)


def solution(mesh):
    return jax.shard_map(
        shards,
        mesh=mesh,
        in_specs=(P("depth", "tile", None), P("depth", "tile", None), P(), P(), P()),
        out_specs=(P(None, ("tile", "depth"), None), P(("tile", "depth"), None)),
        check_vma=False,
    )
```

profile of v0, /device:TPU:64, one launch (start us, length us, event | category | flops | bytes accessed | tf_op | source)
XLA Modules:
  0.0 293.7 jit_solution(9538200003306940795)
XLA Ops:
  7.2 1.1 fusion.12
  8.4 1.9 collective-permute-start
  10.3 3.6 %collective-permute-start.1 = (bf16[16,1,1024]{2,1,0:T(2,128)(2,1)S(1)}, bf16[16,1,1024]{2,1,0:T(2,128)(2,1)S(1)}, u32[]{:S(2)}, u32[]{:S(2)}) collective-permute-start(bf16[16,1,1024]{2,1,0:T(2,128)(2,1)S(1)} %get-tuple-element.20), channel_id=1, source_target_pairs={{32,0},{64,32},{96,64},{128,96},{160,128},{192,160},{224,192},{256... | collective-permute-start | bytes 98312 | tf_op jit(solution)/shard_map/ppermute | solution.py:17
  13.9 0.8 slice_bitcast_fusion
  14.8 1.3 collective-permute-start.2
  16.1 1.6 fusion.15
  17.7 1.7 maximum_convert_fusion
  19.7 1.7 collective-permute-done.2
  21.7 11.2 %fusion.11 = (f32[32,1024]{1,0:T(8,128)S(1)}, f32[16,32,1024]{2,1,0:T(8,128)}, pred[16,32,1024]{2,1,0:T(8,128)(4,1)S(1)}, pred[16,32,1024]{2,1,0:T(8,128)(4,1)},...) fusion(f32[1,32,1024]{2,1,0:T(8,128)S(1)} %bitcast_convert_fusi, ...), kind=kLoop, calls=%fused_computation.39 | loop fusion | flops 15171584 | bytes 14811168 | tf_op jit(solution)/shard_map/reduce_sum | solution.py:49
  32.9 0.6 convert_element_type.31
  34.5 0.7 fusion.14
  35.2 0.7 fusion.13
  36.6 1.9 fusion.16
  39.4 13.2 %multiply_reduce_fusion.2 = (f32[32,1024]{1,0:T(8,128)S(1)}, f32[16,32,1024]{2,1,0:T(8,128)S(1)}) fusion(pred[16,32,1024]{2,1,0:T(8,128)(4,1)} %get-tuple-element.17, pred[16,32,1024]{2,1,0:T(8,128)(4,1)} %get-tuple-element.16, pred[16,32,1024]{2,1,0:T(8,128)(4,1)} %get-tuple-element.15, pred[16,32,1024]{2,1,0:T(8,128)(4,1)} %get-tuple-element.14, ...), kind=kLoop, calls=%fused_computation.17 | loop fusion | flops 15171584 | bytes 19005472 | tf_op jit(solution)/shard_map/reduce_sum | solution.py:48
  52.8 7.3 %multiply_reduce_fusion.1 = f32[32,1024]{1,0:T(8,128)S(1)} fusion(f32[16,32,1024]{2,1,0:T(8,128)S(1)} %get-tuple-element.7, pred[16,32,1024]{2,1,0:T(8,128)(4,1)S(1)} %copy-done.9, pred[16,32,1024]{2,1,0:T(8,128)(4,1)S(1)} %copy-done.8, pred[16,32,1024]{2,1,0:T(8,128)(4,1)S(1)} %copy-done.7, pred[16,32,1024]{2,1,0:T(8,128)(4,1)S(1)} %copy-done.6, ...), kind=kLoop, calls=%fused_computation.16 | loop fusion | flops 8880128 | bytes 6422560 | tf_op jit(solution)/shard_map/reduce_sum | solution.py:48
  60.1 7.3 %multiply_reduce_fusion = f32[32,1024]{1,0:T(8,128)S(1)} fusion(f32[16,32,1024]{2,1,0:T(8,128)S(1)} %get-tuple-element.7, pred[16,32,1024]{2,1,0:T(8,128)(4,1)S(1)} %copy-done.9, pred[16,32,1024]{2,1,0:T(8,128)(4,1)S(1)} %copy-done.8, pred[16,32,1024]{2,1,0:T(8,128)(4,1)S(1)} %copy-done.7, pred[16,32,1024]{2,1,0:T(8,128)(4,1)S(1)} %copy-done.6, ...), kind=kLoop, calls=%fused_computation.15 | loop fusion | flops 8880128 | bytes 6422560 | tf_op jit(solution)/shard_map/reduce_sum | solution.py:48
  67.7 55.7 %all-gather.3.cloned.1.call-done = bf16[1024,1024]{1,0:T(8,128)(2,1)} async-done(((bf16[32,1024]{1,0:T(8,128)(2,1)}), bf16[1024,1024]{1,0:T(8,128)(2,1)}) %all-gather.3.cloned.1.call-update) | async-done | bytes 2097168 | tf_op jit(solution)/shard_map/all_gather | solution.py:65
  123.3 2.1 fusion
  125.9 1.0 pad_maximum_fusion
  126.9 1.3 dynamic-slice
  128.3 154.6 %all-reduce.4.cloned.1.call-done = f32[32,4,1024]{2,1,0:T(4,128)} async-done(((f32[32,4,1024]{2,1,0:T(4,128)}), f32[32,4,1024]{2,1,0:T(4,128)}) %all-reduce.4.cloned.1.call-update) | async-done | bytes 524304
  282.8 1.4 dynamic-slice_bitcast_fusion
  284.2 0.6 copy.8
  284.8 2.0 subtract_bitcast_fusion
  (43 shorter events, 3.8 us)
Async XLA Ops:
  7.2 116.2 %all-gather.3.cloned.1.call-start = ((), (), s32[]{:S(2)}) async-start(), calls=%async_computation | async-start | bytes 2162688 | tf_op jit(solution)/shard_map/all_gather | solution.py:65
  8.4 9.3 %collective-permute-start = (bf16[16,1,1024]{2,1,0:T(2,128)(2,1)S(1)}, bf16[16,1,1024]{2,1,0:T(2,128)(2,1)S(1)}, u32[]{:S(2)}, u32[]{:S(2)}) collective-permute-start(bf16[16,1,1024]{2,1,0:T(2,128)(2,1)S(1)} %get-tuple-element.19), channel_id=1, source_target_pairs={{0,32},{32,64},{64,96},{96,128},{128,160},{160,192},{192,224},{224... | collective-permute-start | bytes 98312 | tf_op jit(solution)/shard_map/ppermute | solution.py:16
  10.3 7.4 %collective-permute-start.1 = (bf16[16,1,1024]{2,1,0:T(2,128)(2,1)S(1)}, bf16[16,1,1024]{2,1,0:T(2,128)(2,1)S(1)}, u32[]{:S(2)}, u32[]{:S(2)}) collective-permute-start(bf16[16,1,1024]{2,1,0:T(2,128)(2,1)S(1)} %get-tuple-element.20), channel_id=1, source_target_pairs={{32,0},{64,32},{96,64},{128,96},{160,128},{192,160},{224,192},{256... | collective-permute-start | bytes 98312 | tf_op jit(solution)/shard_map/ppermute | solution.py:17
  14.8 6.6 %collective-permute-start.2 = (bf16[32,1024]{1,0:T(8,128)(2,1)S(1)}, bf16[32,1024]{1,0:T(8,128)(2,1)S(1)}, u32[]{:S(2)}, u32[]{:S(2)}) collective-permute-start(bf16[32,1024]{1,0:T(8,128)(2,1)S(1)} %slice_bitcast_fusion), channel_id=1, source_target_pairs={{1,0},{2,1},{3,2},{4,3},{5,4},{6,5},{7,6},{8,7},{9,8},{10,9},{11,1... | collective-permute-start | bytes 196616 | tf_op jit(solution)/shard_map/ppermute | solution.py:25
  19.4 2.3 copy-start.10
  19.7 13.3 %copy-start.1 = (f32[15,32,1024]{2,1,0:T(8,128)}, f32[15,32,1024]{2,1,0:T(8,128)S(1)}, u32[]{:S(2)}) copy-start(f32[15,32,1024]{2,1,0:T(8,128)S(1)} %slice.174) | copy-start | bytes 5898244
  21.7 12.1 %copy-start.12 = (s32[32]{0:T(128)S(1)}, s32[32]{0:T(128)}, u32[]{:S(2)}) copy-start(s32[32]{0:T(128)} %param.9) | copy-start | bytes 388
  21.7 12.8 %copy-start.11 = (f32[3,8]{1,0:T(4,128)S(1)}, f32[3,8]{1,0:T(4,128)}, u32[]{:S(2)}) copy-start(f32[3,8]{1,0:T(4,128)} %param.7) | copy-start | bytes 292
  33.6 249.3 %all-reduce.4.cloned.1.call-start = ((), (), s32[]{:S(2)}) async-start(), calls=%async_computation.1 | async-start | bytes 1048576
  36.6 2.2 copy-start
  36.6 2.8 copy-start.2
  39.4 13.3 %copy-start.3 = (pred[16,32,1024]{2,1,0:T(8,128)(4,1)S(1)}, pred[16,32,1024]{2,1,0:T(8,128)(4,1)}, u32[]{:S(2)}) copy-start(pred[16,32,1024]{2,1,0:T(8,128)(4,1)} %get-tuple-element.11) | copy-start | bytes 1572868
  39.4 13.3 %copy-start.4 = (pred[16,32,1024]{2,1,0:T(8,128)(4,1)S(1)}, pred[16,32,1024]{2,1,0:T(8,128)(4,1)}, u32[]{:S(2)}) copy-start(pred[16,32,1024]{2,1,0:T(8,128)(4,1)} %get-tuple-element.12) | copy-start | bytes 1572868
  39.4 13.3 %copy-start.5 = (pred[16,32,1024]{2,1,0:T(8,128)(4,1)S(1)}, pred[16,32,1024]{2,1,0:T(8,128)(4,1)}, u32[]{:S(2)}) copy-start(pred[16,32,1024]{2,1,0:T(8,128)(4,1)} %get-tuple-element.13) | copy-start | bytes 1572868
  39.4 13.3 %copy-start.6 = (pred[16,32,1024]{2,1,0:T(8,128)(4,1)S(1)}, pred[16,32,1024]{2,1,0:T(8,128)(4,1)}, u32[]{:S(2)}) copy-start(pred[16,32,1024]{2,1,0:T(8,128)(4,1)} %get-tuple-element.14) | copy-start | bytes 1572868
  39.4 13.3 %copy-start.7 = (pred[16,32,1024]{2,1,0:T(8,128)(4,1)S(1)}, pred[16,32,1024]{2,1,0:T(8,128)(4,1)}, u32[]{:S(2)}) copy-start(pred[16,32,1024]{2,1,0:T(8,128)(4,1)} %get-tuple-element.15) | copy-start | bytes 1572868
  39.4 13.3 %copy-start.8 = (pred[16,32,1024]{2,1,0:T(8,128)(4,1)S(1)}, pred[16,32,1024]{2,1,0:T(8,128)(4,1)}, u32[]{:S(2)}) copy-start(pred[16,32,1024]{2,1,0:T(8,128)(4,1)} %get-tuple-element.16) | copy-start | bytes 1572868
  39.4 13.3 %copy-start.9 = (pred[16,32,1024]{2,1,0:T(8,128)(4,1)S(1)}, pred[16,32,1024]{2,1,0:T(8,128)(4,1)}, u32[]{:S(2)}) copy-start(pred[16,32,1024]{2,1,0:T(8,128)(4,1)} %get-tuple-element.17) | copy-start | bytes 1572868
Sparse Core Ops, SparseCore 0:
  33.7 89.5 all-gather.2
  127.1 155.7 all-reduce.3
where the time goes:
time: 294 us
  waiting for transfers between devices  212 us (72%)
  other arithmetic  49.5 us (17%)
  between operations  14.3 us (5%)
  local copies, waits for them, and re-layouts  10.8 us (4%)
  starting transfers between devices  7.1 us (2%)
    unnamed x3, waiting for transfers between devices  155 us
    all_gather x1, waiting for transfers between devices, shards(): lax.all_gather(thick[None].astype(jnp.bfloat16), 'depth', axis=0, tiled=T...  55.7 us
    reduce_sum x3, other arithmetic, slab_terms(): jnp.sum(colours[channel] * weight, 0)  27.8 us
    reduce_sum x1, other arithmetic, slab_terms(): return (image, jnp.sum(thick, 0))  11.2 us
  transfers between devices with their start and end apart: 5, of which 3 were waited for; matrix products, arithmetic and copies ran while one was open for 13% of the time, Pallas kernels for 0%

commit v1 on v0

v1 whole, which is shorter than its diff:
```python
import functools
import jax
import jax.numpy as jnp
from jax import lax
from jax.experimental import pallas as pl
from jax.experimental.pallas import tpu as pltpu
from jax.sharding import PartitionSpec as P

MAT = 8
LOG2E = 1.4426950408889634
IMAGE_GAIN = 64.0
THICK_GAIN = 128.0


def power16(x):
    x = x * x
    x = x * x
    x = x * x
    return x * x


def root16(x):
    return jnp.exp2(jnp.log2(x) * 0.0625)


def lookup(table, index):
    return jnp.take_along_axis(table, index, axis=1, mode="promise_in_bounds")


def lane_table(read):
    lane = lax.broadcasted_iota(jnp.int32, (8, 128), 1)
    table = jnp.zeros((8, 128), jnp.float32)
    for m in range(MAT):
        table = jnp.where(lane == m, read(m), table)
    return table


def slab_kernel(dens, mats, above, below, after, emit, absorb, out, field, turned):
    cells, rows, cols = dens.shape
    tiles = cols // 128
    for k in range(cells):
        field[k, pl.ds(8, rows), :] = dens[k].astype(jnp.float32)
    field[cells, pl.ds(8, rows), :] = after[...].astype(jnp.float32)
    up = above[...].astype(jnp.float32)
    down = below[...].astype(jnp.float32)
    for k in range(cells):
        field[k, pl.ds(7, 1), :] = up[k : k + 1]
        field[k, pl.ds(8 + rows, 1), :] = down[k : k + 1]
    emits = [lane_table(lambda m, c=c: emit[c, m] * 0.5) for c in range(3)]
    absorbs = lane_table(lambda m: absorb[m] * (0.25 * LOG2E))
    column = lax.broadcasted_iota(jnp.int32, (8, cols), 1)
    first, last = column == 0, column == cols - 1
    for r in range(rows // 8):
        at = 8 + 8 * r

        def layer(k, carry):
            here, inside, red, green, blue = carry
            nxt = field[k + 1, pl.ds(at, 8), :]
            grad = field[k, pl.ds(at + 1, 8), :] - field[k, pl.ds(at - 1, 8), :]
            right = jnp.where(last, 0.0, pltpu.roll(here, cols - 1, 1))
            left = jnp.where(first, 0.0, pltpu.roll(here, 1, 1))
            shade = 0.6 + 0.4 * jnp.tanh(grad + (right - left))
            twice = here + nxt
            weight = twice * shade * jnp.exp2(-inside)
            index = mats[k, pl.ds(8 * r, 8), :]
            pieces = [index[:, 128 * j : 128 * (j + 1)] for j in range(tiles)]
            look = lambda table: jnp.concatenate([lookup(table, p) for p in pieces], 1)
            inside = inside + look(absorbs) * (twice * twice)
            red, green, blue = (
                total + look(table) * weight
                for total, table in zip((red, green, blue), emits)
            )
            return (nxt, inside, red, green, blue)

        zero = jnp.zeros((8, cols), jnp.float32)
        start = (field[0, pl.ds(at, 8), :], zero, zero, zero, zero)
        _, inside, red, green, blue = lax.fori_loop(0, cells, layer, start, unroll=2)
        coded = [power16(v * IMAGE_GAIN) for v in (red, green, blue)]
        coded.append(power16(inside * (THICK_GAIN / LOG2E)))
        for c, value in enumerate(coded):
            for j in range(tiles):
                turned[pl.ds(8 * r * 32 + c * tiles + j, 8, stride=32), :] = value[
                    :, 128 * j : 128 * (j + 1)
                ]
    for i in range(rows):
        out[i] = turned[pl.ds(32 * i, 32), :].astype(jnp.bfloat16)


def final_kernel(order, parts, colour, opacity):
    slabs = parts.shape[0]
    front = jnp.zeros((8, 128), jnp.float32)
    totals = [jnp.zeros((8, 128), jnp.float32) for _ in range(3)]
    for rank in range(slabs):
        slab = order[rank]
        value = root16(parts[slab].astype(jnp.float32))
        through = jnp.exp2(-front)
        for c in range(3):
            totals[c] = totals[c] + value[8 * c : 8 * c + 8] * through
        front = front + value[24:32] * (LOG2E / THICK_GAIN)
    for c in range(3):
        colour[c] = totals[c] * (1.0 / IMAGE_GAIN)
    opacity[...] = 1.0 - jnp.exp2(-front)


def shards(density, materials, emit_table, absorb_table, depth_order):
    cells, rows, cols = density.shape
    tiles, slabs = lax.axis_size("tile"), lax.axis_size("depth")
    up = [(i, i + 1) for i in range(tiles - 1)]
    down = [(i + 1, i) for i in range(tiles - 1)]
    nearer = [(i + 1, i) for i in range(slabs - 1)]
    above = lax.ppermute(density[:, rows - 1], "tile", up)
    below = lax.ppermute(density[:, 0], "tile", down)
    after = lax.ppermute(density[0], "depth", nearer)
    vmem = pl.BlockSpec(memory_space=pltpu.VMEM)
    smem = pl.BlockSpec(memory_space=pltpu.SMEM)
    parts = pl.pallas_call(
        slab_kernel,
        out_shape=jax.ShapeDtypeStruct((rows, 32, 128), jnp.bfloat16),
        in_specs=[vmem] * 5 + [smem] * 2,
        out_specs=vmem,
        scratch_shapes=[
            pltpu.VMEM((cells + 1, rows + 16, cols), jnp.float32),
            pltpu.VMEM((rows * 32, 128), jnp.float32),
        ],
        compiler_params=pltpu.CompilerParams(vmem_limit_bytes=32 << 20),
    )(density, materials, above, below, after, emit_table, absorb_table)
    parts = lax.all_to_all(parts, "depth", 0, 0, tiled=True)
    colour, opacity = pl.pallas_call(
        final_kernel,
        out_shape=(
            jax.ShapeDtypeStruct((3, 8, 128), jnp.float32),
            jax.ShapeDtypeStruct((8, 128), jnp.float32),
        ),
        in_specs=[smem, vmem],
        out_specs=(vmem, vmem),
    )(depth_order, parts)
    return colour.reshape(3, 1, cols), opacity.reshape(1, cols)


def solution(mesh):
    return jax.shard_map(
        shards,
        mesh=mesh,
        in_specs=(P("depth", "tile", None), P("depth", "tile", None), P(), P(), P()),
        out_specs=(P(None, ("tile", "depth"), None), P(("tile", "depth"), None)),
        check_vma=False,
    )
```

time: 294 us -> 53.5 us (0.18)
  the two profiles are of different devices: /device:TPU:64 before, /device:TPU:201 now
where the time goes in v1:
time: 53.5 us; the launch traced here: 53.1 us
  blocking collectives  19.9 us (37%)
  Pallas kernels  11.8 us (22%)
  starting transfers between devices  10 us (19%)
  local copies, waits for them, and re-layouts  6.17 us (12%)
  waiting for transfers between devices  4.51 us (8%)
  between operations  0.69 us (1%)
    all_to_all x1, blocking collectives, shards(): parts = lax.all_to_all(parts, 'depth', 0, 0, tiled=True)  19.9 us
    pallas_call x1, Pallas kernels, shards(): pl.pallas_call(slab_kernel, out_shape=jax.ShapeDtypeStruct((rows, 32, 128...  10.1 us
    ppermute x1, starting transfers between devices, shards(): above = lax.ppermute(density[:, rows - 1], 'tile', up)  6.05 us
    ppermute x1, waiting for transfers between devices, shards(): below = lax.ppermute(density[:, 0], 'tile', down)  4.51 us
    unnamed x10, local copies, waits for them, and re-layouts  4.18 us
    ppermute x1, starting transfers between devices, shards(): after = lax.ppermute(density[0], 'depth', nearer)  2.07 us
    ppermute x1, starting transfers between devices, shards(): below = lax.ppermute(density[:, 0], 'tile', down)  1.92 us
    pallas_call x1, Pallas kernels, shards(): pl.pallas_call(final_kernel, out_shape=(jax.ShapeDtypeStruct((3, 8, 128),...  1.73 us
  transfers between devices with their start and end apart: 3, of which 1 were waited for; matrix products, arithmetic and copies ran while one was open for 2% of the time, Pallas kernels for 0%

profile of v1, /device:TPU:201, one launch (start us, length us, event | category | flops | bytes accessed | tf_op | source)
XLA Modules:
  0.0 53.1 jit_solution(329983081001038797)
XLA Ops:
  0.6 0.8 %slice_bitcast_fusion = bf16[32,1024]{1,0:T(8,128)(2,1)S(1)} fusion(bf16[16,32,1024]{2,1,0:T(8,128)(2,1)} %dens.1), kind=kLoop, calls=%fused_computation | loop fusion | bytes 131072 | tf_op jit(solution)/shard_map/squeeze | solution.py:113
  1.5 2.1 %collective-permute-start.2 = (bf16[32,1024]{1,0:T(8,128)(2,1)S(1)}, bf16[32,1024]{1,0:T(8,128)(2,1)S(1)}, u32[]{:S(2)}, u32[]{:S(2)}) collective-permute-start(bf16[32,1024]{1,0:T(8,128)(2,1)S(1)} %slice_bitcast_fusion), channel_id=1, source_target_pairs={{1,0},{2,1},{3,2},{4,3},{5,4},{6,5},{7,6},{8,7},{9,8},{10,9},{11,1... | collective-permute-start | bytes 196616 | tf_op jit(solution)/shard_map/ppermute | solution.py:113
  3.5 1.1 %fusion = (bf16[16,1,1024]{2,1,0:T(2,128)(2,1)S(1)}, bf16[16,1,1024]{2,1,0:T(2,128)(2,1)S(1)}) fusion(bf16[16,32,1024]{2,1,0:T(8,128)(2,1)} %dens.1), kind=kLoop, calls=%fused_computation.3 | loop fusion | bytes 131072 | tf_op jit(solution)/shard_map/slice | solution.py:112
  4.7 6.1 %collective-permute-start = (bf16[16,1024]{1,0:T(8,128)(2,1)S(1)}, bf16[16,1024]{1,0:T(8,128)(2,1)S(1)}, u32[]{:S(2)}, u32[]{:S(2)}) collective-permute-start(bf16[16,1024]{1,0:T(8,128)(2,1)S(1)} %bitcast.10), channel_id=1, source_target_pairs={{0,32},{32,64},{64,96},{96,128},{128,160},{160,192},{192,224},{224... | collective-permute-start | bytes 98312 | tf_op jit(solution)/shard_map/ppermute | solution.py:111
  10.8 1.9 %collective-permute-start.1 = (bf16[16,1024]{1,0:T(8,128)(2,1)S(1)}, bf16[16,1024]{1,0:T(8,128)(2,1)S(1)}, u32[]{:S(2)}, u32[]{:S(2)}) collective-permute-start(bf16[16,1024]{1,0:T(8,128)(2,1)S(1)} %bitcast.11), channel_id=1, source_target_pairs={{32,0},{64,32},{96,64},{128,96},{160,128},{192,160},{224,192},{256... | collective-permute-start | bytes 98312 | tf_op jit(solution)/shard_map/ppermute | solution.py:112
  12.7 0.0 collective-permute-done.above
  12.7 4.5 %collective-permute-done.1.below = bf16[16,1024]{1,0:T(8,128)(2,1)S(1)} collective-permute-done((bf16[16,1024]{1,0:T(8,128)(2,1)S(1)}, bf16[16,1024]{1,0:T(8,128)(2,1)S(1)}, u32[]{:S(2)}, u32[]{:S(2)}) %collective-permute-start.1) | collective-permute-done | bytes 32800 | tf_op jit(solution)/shard_map/ppermute | solution.py:112
  17.2 0.0 collective-permute-done.2.after
  17.2 0.0 copy-start
  17.2 1.6 %copy-done = s32[16,32,1024]{2,1,0:T(8,128)S(1)} copy-done((s32[16,32,1024]{2,1,0:T(8,128)S(1)}, s32[16,32,1024]{2,1,0:T(8,128)}, u32[]{:S(2)}) %copy-start) | copy-done | bytes 2097176
  18.8 0.0 copy-start.1
  18.8 1.2 %copy-done.1 = bf16[16,32,1024]{2,1,0:T(8,128)(2,1)S(1)} copy-done((bf16[16,32,1024]{2,1,0:T(8,128)(2,1)S(1)}, bf16[16,32,1024]{2,1,0:T(8,128)(2,1)}, u32[]{:S(2)}) %copy-start.1) | copy-done | bytes 1048600
  20.1 0.0 copy-start.2
  20.1 0.7 %copy-done.2 = f32[3,8]{1,0:T(4,128)S(1)} copy-done((f32[3,8]{1,0:T(4,128)S(1)}, f32[3,8]{1,0:T(4,128)}, u32[]{:S(2)}) %copy-start.2) | copy-done | bytes 120
  20.7 0.0 copy-start.3
  20.7 0.7 %copy-done.3 = f32[8]{0:T(128)S(1)} copy-done((f32[8]{0:T(128)S(1)}, f32[8]{0:T(128)}, u32[]{:S(2)}) %copy-start.3) | copy-done | bytes 56
  21.4 10.1 %shard_map.68 = bf16[32,32,128]{2,1,0:T(8,128)(2,1)S(1)} custom-call(bf16[16,32,1024]{2,1,0:T(8,128)(2,1)S(1)} %copy-done.1, s32[16,32,1024]{2,1,0:T(8,128)S(1)} %copy-done, bf16[16,1024]{1,0:T(8,128)(2,1)S(1)} %collective-permute-done.above, bf16[16,1024]{1,0:T(8,128)(2,1)S(1)} %collective-permute-done.1.below, ...), custom_call_target="tpu_custom_call" | custom-call | tf_op jit(solution)/shard_map/pallas_call | solution.py:116
  31.5 19.9 %all_to_all.5.parts = bf16[32,32,128]{2,1,0:T(8,128)(2,1)} all-to-all(bf16[32,32,128]{2,1,0:T(8,128)(2,1)S(1)} %shard_map.68), channel_id=1, replica_groups=mesh['tile'=16,'depth'=32] {'depth'}, dimensions={0} | all-to-all | bytes 524288 | tf_op jit(solution)/shard_map/all_to_all | solution.py:127
  51.4 1.7 %shard_map.69 = (f32[3,8,128]{2,1,0:T(8,128)}, f32[8,128]{1,0:T(8,128)}) custom-call(s32[32]{0:T(128)} %order.1, bf16[32,32,128]{2,1,0:T(8,128)(2,1)} %all_to_all.5.parts), custom_call_target="tpu_custom_call" | custom-call | tf_op jit(solution)/shard_map/pallas_call | solution.py:128
  (2 shorter events, 0.0 us)
Async XLA Ops:
  1.5 15.8 %collective-permute-start.2 = (bf16[32,1024]{1,0:T(8,128)(2,1)S(1)}, bf16[32,1024]{1,0:T(8,128)(2,1)S(1)}, u32[]{:S(2)}, u32[]{:S(2)}) collective-permute-start(bf16[32,1024]{1,0:T(8,128)(2,1)S(1)} %slice_bitcast_fusion), channel_id=1, source_target_pairs={{1,0},{2,1},{3,2},{4,3},{5,4},{6,5},{7,6},{8,7},{9,8},{10,9},{11,1... | collective-permute-start | bytes 196616 | tf_op jit(solution)/shard_map/ppermute | solution.py:113
  4.7 8.0 %collective-permute-start = (bf16[16,1024]{1,0:T(8,128)(2,1)S(1)}, bf16[16,1024]{1,0:T(8,128)(2,1)S(1)}, u32[]{:S(2)}, u32[]{:S(2)}) collective-permute-start(bf16[16,1024]{1,0:T(8,128)(2,1)S(1)} %bitcast.10), channel_id=1, source_target_pairs={{0,32},{32,64},{64,96},{96,128},{128,160},{160,192},{192,224},{224... | collective-permute-start | bytes 98312 | tf_op jit(solution)/shard_map/ppermute | solution.py:111
  10.8 6.4 %collective-permute-start.1 = (bf16[16,1024]{1,0:T(8,128)(2,1)S(1)}, bf16[16,1024]{1,0:T(8,128)(2,1)S(1)}, u32[]{:S(2)}, u32[]{:S(2)}) collective-permute-start(bf16[16,1024]{1,0:T(8,128)(2,1)S(1)} %bitcast.11), channel_id=1, source_target_pairs={{32,0},{64,32},{96,64},{128,96},{160,128},{192,160},{224,192},{256... | collective-permute-start | bytes 98312 | tf_op jit(solution)/shard_map/ppermute | solution.py:112
  17.2 1.6 %copy-start = (s32[16,32,1024]{2,1,0:T(8,128)S(1)}, s32[16,32,1024]{2,1,0:T(8,128)}, u32[]{:S(2)}) copy-start(s32[16,32,1024]{2,1,0:T(8,128)} %mats.1) | copy-start | bytes 6291460
  18.8 1.2 %copy-start.1 = (bf16[16,32,1024]{2,1,0:T(8,128)(2,1)S(1)}, bf16[16,32,1024]{2,1,0:T(8,128)(2,1)}, u32[]{:S(2)}) copy-start(bf16[16,32,1024]{2,1,0:T(8,128)(2,1)} %dens.1) | copy-start | bytes 3145732
  20.1 0.7 %copy-start.2 = (f32[3,8]{1,0:T(4,128)S(1)}, f32[3,8]{1,0:T(4,128)}, u32[]{:S(2)}) copy-start(f32[3,8]{1,0:T(4,128)} %emit.1) | copy-start | bytes 292
  20.7 0.7 %copy-start.3 = (f32[8]{0:T(128)S(1)}, f32[8]{0:T(128)}, u32[]{:S(2)}) copy-start(f32[8]{0:T(128)} %absorb.1) | copy-start | bytes 100

commit v2 on v1

v2 whole, which is shorter than its diff:
```python
import jax
import jax.numpy as jnp
from jax import lax
from jax.experimental import pallas as pl
from jax.experimental.pallas import tpu as pltpu
from jax.sharding import PartitionSpec as P

MAT = 8
LOG2E = 1.4426950408889634
IMAGE_GAIN = 64.0
THICK_GAIN = 128.0
HALF = 4
PITCH = 48


def power16(x):
    x = x * x
    x = x * x
    x = x * x
    return x * x


def root16(x):
    return jnp.exp2(jnp.log2(x) * 0.0625)


def lookup(table, index):
    return jnp.take_along_axis(table, index, axis=0, mode="promise_in_bounds")


def row_table(read):
    row = lax.broadcasted_iota(jnp.int32, (8, 128), 0)
    table = jnp.zeros((8, 128), jnp.float32)
    for m in range(MAT):
        table = jnp.where(row == m, read(m), table)
    return table


def edge_kernel(dens_h, emit_h, absorb_h, dens, layer, near, far, tables, edges, emit, absorb, sems):
    cells, rows, cols = dens.shape
    load = pltpu.make_async_copy(dens_h, dens, sems.at[0])
    load.start()
    load_emit = pltpu.make_async_copy(emit_h, emit, sems.at[1])
    load_emit.start()
    load_absorb = pltpu.make_async_copy(absorb_h, absorb, sems.at[2])
    load_absorb.start()
    load_absorb.wait()
    load_emit.wait()
    tables[0] = row_table(lambda m: absorb[m] * (-0.25 * LOG2E))
    for c in range(3):
        tables[1 + c] = row_table(lambda m, c=c: emit[c, m] * (0.2 * IMAGE_GAIN))
    load.wait()
    layer[...] = dens[0]
    for k in range(cells):
        edges[0, pl.ds(k, 1), :] = dens[k, 0:1, :].astype(jnp.float32)
        edges[1, pl.ds(k, 1), :] = dens[k, rows - 1 : rows, :].astype(jnp.float32)
    odd = lax.axis_index("tile") % 2
    first, last = edges[0], edges[1]
    near[...] = jnp.where(odd == 1, first, last).astype(jnp.bfloat16)
    far[...] = jnp.where(odd == 1, last, first).astype(jnp.bfloat16)


def body_kernel(dens, mats_h, tables, sums, final, border, mats, field, sems):
    cells, rows, cols = dens.shape
    tiles, strips = cols // 128, rows // 8
    loads = []
    for r in range(strips):
        part = pl.ds(8 * r, 8)
        loads.append(pltpu.make_async_copy(mats_h.at[:, part, :], mats.at[:, part, :], sems.at[r]))
        loads[-1].start()
    table = [tables[q] for q in range(4)]
    lane = lax.broadcasted_iota(jnp.int32, (8, 128), 1)
    row = lax.broadcasted_iota(jnp.int32, (8, 128), 0)
    for k in range(cells):
        layer = dens[k].astype(jnp.float32)
        for j in range(tiles):
            field[pl.ds((k * tiles + j) * PITCH + 8, rows), :] = layer[:, 128 * j : 128 * (j + 1)]

    def cell(k, j, at, count=8):
        return field[pl.ds((k * tiles + j) * PITCH + 8 + at, count), :]

    def along(row_number, half, j):
        start = (8 * half * tiles + j) * PITCH + 8 + row_number
        return field[pl.ds(start, 8, stride=tiles * PITCH), :]

    zero = jnp.zeros((8, 128), jnp.float32)

    def across(before, f, behind):
        left = pltpu.roll(jnp.where(lane == 127, before, f), 1, 1)
        right = pltpu.roll(jnp.where(lane == 0, behind, f), 127, 1)
        return right - left

    for r in range(strips):
        loads[r].wait()
        at = 8 * r
        for j0 in range(0, tiles, HALF):
            js = range(j0, j0 + HALF)
            here = [cell(0, j, at) for j in js]
            inside, red, green, blue = ([zero] * HALF for _ in range(4))
            for k in range(cells):
                last = k == cells - 1
                nxt = here if last else [cell(k + 1, j, at) for j in js]
                before = cell(k, j0 - 1, at) if j0 else zero
                behind = cell(k, j0 + HALF, at) if j0 + HALF < tiles else zero
                wide = [before, *here, behind]
                for n, j in enumerate(js):
                    f = here[n]
                    upper, lower = cell(k, j, at - 1), cell(k, j, at + 1)
                    if r == 0:
                        upper = jnp.where(row == 0, 0.0, upper)
                    if r == strips - 1:
                        lower = jnp.where(row == 7, 0.0, lower)
                    shade = 1.5 + jnp.tanh((lower - upper) + across(wide[n], f, wide[n + 2]))
                    index = mats[k, pl.ds(at, 8), 128 * j : 128 * (j + 1)]
                    found = [lookup(t, index) for t in table]
                    spot = pl.ds((r * tiles + j) * 8, 8)
                    if last:
                        for q in range(4):
                            final[q, spot, :] = found[q]
                            sums[q, spot, :] = (inside, red, green, blue)[q][n]
                        final[4, spot, :] = shade * jnp.exp2(inside[n])
                        final[5, spot, :] = f
                        continue
                    twice = f + nxt[n]
                    weight = twice * shade * jnp.exp2(inside[n])
                    inside[n] = inside[n] + found[0] * (twice * twice)
                    red[n] = red[n] + found[1] * weight
                    green[n] = green[n] + found[2] * weight
                    blue[n] = blue[n] + found[3] * weight
                here = nxt

    for e, (own, inner) in enumerate(((0, 1), (rows - 1, rows - 2))):
        sign = 1.0 if e == 0 else -1.0
        f = [[along(own, h, j) for j in range(tiles)] for h in range(2)]
        for j in range(tiles):
            carried = jnp.zeros((1, 128), jnp.float32)
            for h in range(2):
                before = f[h][j - 1] if j else zero
                behind = f[h][j + 1] if j + 1 < tiles else zero
                grad = sign * along(inner, h, j) + across(before, f[h][j], behind)
                behind_first = f[1][j][0:1] if h == 0 else jnp.zeros((1, 128), jnp.float32)
                nxt = pltpu.roll(f[h][j], 7, 0)
                twice = f[h][j] + jnp.where(row == 7, behind_first, nxt)
                index = jnp.concatenate(
                    [mats[8 * h + i, own : own + 1, 128 * j : 128 * (j + 1)] for i in range(8)], 0
                )
                found = [lookup(t, index) for t in table]
                thick = found[0] * twice * twice
                total = thick
                for step in (1, 2, 4):
                    total = total + jnp.where(row >= step, pltpu.roll(total, step, 0), 0.0)
                through = jnp.exp2(total - thick + carried)
                carried = carried + total[7:8]
                spot = (pl.ds(8 * h, 8), pl.ds(128 * j, 128))
                border[e, 0, *spot] = grad
                border[e, 1, *spot] = twice
                for c in range(3):
                    border[e, 2 + c, *spot] = found[1 + c] * through


def join_kernel(sums, final, border, near, far, after, out):
    cells, cols = near.shape
    rows = after.shape[0]
    tiles, strips = cols // 128, rows // 8
    odd = lax.axis_index("tile") % 2
    near_rows, far_rows = near[...].astype(jnp.float32), far[...].astype(jnp.float32)
    up = jnp.where(odd == 1, near_rows, far_rows)
    down = jnp.where(odd == 1, far_rows, near_rows)
    behind = after[...].astype(jnp.float32)
    cell = lax.broadcasted_iota(jnp.int32, (cells, cols), 0)
    row = lax.broadcasted_iota(jnp.int32, (8, 128), 0)
    outer = []
    for e, halo in enumerate((-up, down)):
        own = behind[0:1] if e == 0 else behind[rows - 1 : rows]
        twice = border[e, 1] + jnp.where(cell == cells - 1, own, 0.0)
        weight = twice * (1.5 + jnp.tanh(border[e, 0] + halo))
        outer.append([jnp.sum(border[e, 2 + c] * weight, 0, keepdims=True) for c in range(3)])
    a = lax.broadcasted_iota(jnp.int32, (256, 256), 0)
    b = lax.broadcasted_iota(jnp.int32, (256, 256), 1)
    turn = jnp.where((a // 32 == b % 8) & (a % 32 == b // 8), 1.0, 0.0).astype(jnp.bfloat16)
    stacks = []
    for r in range(strips):
        block = [[None] * tiles for _ in range(4)]
        for j in range(tiles):
            spot = pl.ds((r * tiles + j) * 8, 8)
            part = slice(128 * j, 128 * (j + 1))
            twice = final[5, spot, :] + behind[8 * r : 8 * r + 8, part]
            inside = sums[0, spot, :] + final[0, spot, :] * (twice * twice)
            weight = twice * final[4, spot, :]
            for c in range(3):
                value = sums[1 + c, spot, :] + final[1 + c, spot, :] * weight
                if r == 0:
                    value = jnp.where(row == 0, outer[0][c][:, part], value)
                if r == strips - 1:
                    value = jnp.where(row == 7, outer[1][c][:, part], value)
                block[c][j] = power16(value)
            block[3][j] = power16(inside * (-THICK_GAIN / LOG2E))
        stacks.append(jnp.concatenate([v for c in block for v in c], 0).astype(jnp.bfloat16))
    moved = jnp.dot(turn, jnp.concatenate(stacks, 1), preferred_element_type=jnp.float32)
    for r in range(strips):
        strip = moved[:, 128 * r : 128 * (r + 1)].astype(jnp.bfloat16)
        out[pl.ds(8 * r, 8)] = strip.reshape(8, 32, 128)


def final_kernel(order, parts, colour, opacity):
    slabs = parts.shape[0]
    front = jnp.zeros((8, 128), jnp.float32)
    totals = [jnp.zeros((8, 128), jnp.float32) for _ in range(3)]
    for rank in range(slabs):
        slab = order[rank]
        value = root16(parts[slab].astype(jnp.float32))
        through = jnp.exp2(-front)
        for c in range(3):
            totals[c] = totals[c] + value[8 * c : 8 * c + 8] * through
        front = front + value[24:32] * (LOG2E / THICK_GAIN)
    for c in range(3):
        colour[c] = totals[c] * (1.0 / IMAGE_GAIN)
    opacity[...] = 1.0 - jnp.exp2(-front)


def shards(density, materials, emit_table, absorb_table, depth_order):
    cells, rows, cols = density.shape
    tiles, slabs = lax.axis_size("tile"), lax.axis_size("depth")
    swap = [(i, i ^ 1) for i in range(tiles)]
    cross = [(i, i + 1) for i in range(1, tiles - 1, 2)]
    cross += [(j, i) for i, j in cross]
    nearer = [(i + 1, i) for i in range(slabs - 1)]
    vmem = pl.BlockSpec(memory_space=pltpu.VMEM)
    smem = pl.BlockSpec(memory_space=pltpu.SMEM)
    hbm = pl.BlockSpec(memory_space=pltpu.HBM)
    room = pltpu.CompilerParams(vmem_limit_bytes=32 << 20)
    spots = rows * cols // 128
    dens, layer, near, far, tables = pl.pallas_call(
        edge_kernel,
        out_shape=(
            jax.ShapeDtypeStruct(density.shape, density.dtype),
            jax.ShapeDtypeStruct((rows, cols), density.dtype),
            jax.ShapeDtypeStruct((cells, cols), density.dtype),
            jax.ShapeDtypeStruct((cells, cols), density.dtype),
            jax.ShapeDtypeStruct((4, 8, 128), jnp.float32),
        ),
        in_specs=[hbm] * 3,
        out_specs=(vmem,) * 5,
        scratch_shapes=[
            pltpu.VMEM((2, cells, cols), jnp.float32),
            pltpu.SMEM(emit_table.shape, jnp.float32),
            pltpu.SMEM(absorb_table.shape, jnp.float32),
            pltpu.SemaphoreType.DMA((3,)),
        ],
        compiler_params=room,
    )(density, emit_table, absorb_table)
    after = lax.ppermute(layer, "depth", nearer)
    near = lax.ppermute(near, "tile", swap)
    far = lax.ppermute(far, "tile", cross)
    sums, final, border = pl.pallas_call(
        body_kernel,
        out_shape=(
            jax.ShapeDtypeStruct((4, spots, 128), jnp.float32),
            jax.ShapeDtypeStruct((6, spots, 128), jnp.float32),
            jax.ShapeDtypeStruct((2, 5, cells, cols), jnp.float32),
        ),
        in_specs=[vmem, hbm, vmem],
        out_specs=(vmem,) * 3,
        scratch_shapes=[
            pltpu.VMEM(materials.shape, materials.dtype),
            pltpu.VMEM((cells * (cols // 128) * PITCH, 128), jnp.float32),
            pltpu.SemaphoreType.DMA((rows // 8,)),
        ],
        compiler_params=room,
    )(dens, materials, tables)
    parts = pl.pallas_call(
        join_kernel,
        out_shape=jax.ShapeDtypeStruct((rows, 32, 128), jnp.bfloat16),
        in_specs=[vmem] * 6,
        out_specs=vmem,
        compiler_params=room,
    )(sums, final, border, near, far, after)
    parts = lax.all_to_all(parts, "depth", 0, 0, tiled=True)
    colour, opacity = pl.pallas_call(
        final_kernel,
        out_shape=(
            jax.ShapeDtypeStruct((3, 8, 128), jnp.float32),
            jax.ShapeDtypeStruct((8, 128), jnp.float32),
        ),
        in_specs=[smem, vmem],
        out_specs=(vmem, vmem),
    )(depth_order, parts)
    return colour.reshape(3, 1, cols), opacity.reshape(1, cols)


def solution(mesh):
    return jax.shard_map(
        shards,
        mesh=mesh,
        in_specs=(P("depth", "tile", None), P("depth", "tile", None), P(), P(), P()),
        out_specs=(P(None, ("tile", "depth"), None), P(("tile", "depth"), None)),
        check_vma=False,
    )
```

time: 53.5 us -> 41.1 us (0.77)
  the two profiles are of different devices: /device:TPU:201 before, /device:TPU:265 now
where the time goes in v2:
time: 41.1 us; the launch traced here: 40.8 us
  blocking collectives  22.5 us (55%)
  starting transfers between devices  7.94 us (19%)
  Pallas kernels  5.48 us (13%)
  local copies, waits for them, and re-layouts  4.14 us (10%)
  between operations  0.72 us (2%)
    all_to_all x1, blocking collectives, shards(): parts = lax.all_to_all(parts, 'depth', 0, 0, tiled=True)  22.5 us
    unnamed x8, local copies, waits for them, and re-layouts  4.14 us
    ppermute x1, starting transfers between devices, shards(): far = lax.ppermute(far, 'tile', cross)  3 us
    ppermute x1, starting transfers between devices, shards(): near = lax.ppermute(near, 'tile', swap)  2.86 us
    pallas_call x1, Pallas kernels, shards(): pl.pallas_call(body_kernel, out_shape=(jax.ShapeDtypeStruct((4, spots, 12...  2.52 us
    ppermute x1, starting transfers between devices, shards(): after = lax.ppermute(layer, 'depth', nearer)  2.08 us
    pallas_call x1, Pallas kernels, shards(): pl.pallas_call(final_kernel, out_shape=(jax.ShapeDtypeStruct((3, 8, 128),...  1.73 us
  transfers between devices with their start and end apart: 3, of which 0 were waited for; matrix products, arithmetic and copies ran while one was open for 0% of the time, Pallas kernels for 6%

profile of v2, /device:TPU:265, one launch (start us, length us, event | category | flops | bytes accessed | tf_op | source)
XLA Modules:
  0.0 40.8 jit_solution(13899632829790345156)
XLA Ops:
  0.6 0.0 copy-start.1
  0.6 1.2 %copy-done.1 = bf16[16,32,1024]{2,1,0:T(8,128)(2,1)S(1)} copy-done((bf16[16,32,1024]{2,1,0:T(8,128)(2,1)S(1)}, bf16[16,32,1024]{2,1,0:T(8,128)(2,1)}, u32[]{:S(2)}) %copy-start.1) | copy-done | bytes 1048600
  1.9 0.0 copy-start.2
  1.9 0.7 %copy-done.2 = f32[3,8]{1,0:T(4,128)S(1)} copy-done((f32[3,8]{1,0:T(4,128)S(1)}, f32[3,8]{1,0:T(4,128)}, u32[]{:S(2)}) %copy-start.2) | copy-done | bytes 120
  2.5 0.0 copy-start.3
  2.5 0.7 %copy-done.3 = f32[8]{0:T(128)S(1)} copy-done((f32[8]{0:T(128)S(1)}, f32[8]{0:T(128)}, u32[]{:S(2)}) %copy-start.3) | copy-done | bytes 56
  3.2 0.8 %shard_map.68 = (bf16[16,32,1024]{2,1,0:T(8,128)(2,1)S(1)}, bf16[32,1024]{1,0:T(8,128)(2,1)S(1)}, bf16[16,1024]{1,0:T(8,128)(2,1)S(1)}, bf16[16,1024]{1,0:T(8,128)(2,1)S(1)}, f32[4,8,128]{2,1,0:T(8,128)S(1)}) custom-call(bf16[16,32,1024]{2,1,0:T(8,128)(2,1)S(1)} %copy-done.1, f32[3,8]{1,0:T(4,128)S(1)} %copy-done.2, f32[8]{0:T(128)S(1)} %copy-done.3), custom_call_target="tpu_custom_call" | custom-call | tf_op jit(solution)/shard_map/pallas_call | solution.py:233
  4.0 2.1 %collective-permute-start.2 = (bf16[32,1024]{1,0:T(8,128)(2,1)S(1)}, bf16[32,1024]{1,0:T(8,128)(2,1)S(1)}, u32[]{:S(2)}, u32[]{:S(2)}) collective-permute-start(bf16[32,1024]{1,0:T(8,128)(2,1)S(1)} %get-tuple-element.19), channel_id=1, source_target_pairs={{1,0},{2,1},{3,2},{4,3},{5,4},{6,5},{7,6},{8,7},{9,8},{10,9},{11,1... | collective-permute-start | bytes 196616 | tf_op jit(solution)/shard_map/ppermute | solution.py:252
  6.1 2.9 %collective-permute-start = (bf16[16,1024]{1,0:T(8,128)(2,1)S(1)}, bf16[16,1024]{1,0:T(8,128)(2,1)S(1)}, u32[]{:S(2)}, u32[]{:S(2)}) collective-permute-start(bf16[16,1024]{1,0:T(8,128)(2,1)S(1)} %get-tuple-element.17), channel_id=1, source_target_pairs={{0,32},{32,0},{64,96},{96,64},{128,160},{160,128},{192,224},{224,1... | collective-permute-start | bytes 98312 | tf_op jit(solution)/shard_map/ppermute | solution.py:253
  9.0 3.0 %collective-permute-start.1 = (bf16[16,1024]{1,0:T(8,128)(2,1)S(1)}, bf16[16,1024]{1,0:T(8,128)(2,1)S(1)}, u32[]{:S(2)}, u32[]{:S(2)}) collective-permute-start(bf16[16,1024]{1,0:T(8,128)(2,1)S(1)} %get-tuple-element.18), channel_id=1, source_target_pairs={{32,64},{96,128},{160,192},{224,256},{288,320},{352,384},{416,448}... | collective-permute-start | bytes 98312 | tf_op jit(solution)/shard_map/ppermute | solution.py:254
  12.0 0.0 copy-start
  12.0 1.6 %copy-done = s32[16,32,1024]{2,1,0:T(8,128)S(1)} copy-done((s32[16,32,1024]{2,1,0:T(8,128)S(1)}, s32[16,32,1024]{2,1,0:T(8,128)}, u32[]{:S(2)}) %copy-start) | copy-done | bytes 2097176
  13.6 2.5 %shard_map.69 = (f32[4,256,128]{2,1,0:T(8,128)S(1)}, f32[6,256,128]{2,1,0:T(8,128)S(1)}, f32[2,5,16,1024]{3,2,1,0:T(8,128)S(1)}) custom-call(bf16[16,32,1024]{2,1,0:T(8,128)(2,1)S(1)} %get-tuple-element.12.dens, s32[16,32,1024]{2,1,0:T(8,128)S(1)} %copy-done, f32[4,8,128]{2,1,0:T(8,128)S(1)} %get-tuple-element.13.tables), custom_call_target="tpu_custom_call" | custom-call | tf_op jit(solution)/shard_map/pallas_call | solution.py:255
  16.1 0.0 collective-permute-done.near
  16.1 0.0 collective-permute-done.1.far
  16.1 0.0 collective-permute-done.2.after
  16.1 0.4 %shard_map.70 = bf16[32,32,128]{2,1,0:T(8,128)(2,1)S(1)} custom-call(f32[4,256,128]{2,1,0:T(8,128)S(1)} %get-tuple-element.14.sums, f32[6,256,128]{2,1,0:T(8,128)S(1)} %get-tuple-element.15.final, f32[2,5,16,1024]{3,2,1,0:T(8,128)S(1)} %get-tuple-element.16.border, bf16[16,1024]{1,0:T(8,128)(2,1)S(1)} %collective-permute-done.near, ...), custom_call_target="tpu_custom_call" | custom-call | tf_op jit(solution)/shard_map/pallas_call | solution.py:271
  16.6 22.5 %all_to_all.5.parts = bf16[32,32,128]{2,1,0:T(8,128)(2,1)} all-to-all(bf16[32,32,128]{2,1,0:T(8,128)(2,1)S(1)} %shard_map.70), channel_id=1, replica_groups=mesh['tile'=16,'depth'=32] {'depth'}, dimensions={0} | all-to-all | bytes 524288 | tf_op jit(solution)/shard_map/all_to_all | solution.py:278
  39.0 1.7 %shard_map.71 = (f32[3,8,128]{2,1,0:T(8,128)}, f32[8,128]{1,0:T(8,128)}) custom-call(s32[32]{0:T(128)} %order.1, bf16[32,32,128]{2,1,0:T(8,128)(2,1)} %all_to_all.5.parts), custom_call_target="tpu_custom_call" | custom-call | tf_op jit(solution)/shard_map/pallas_call | solution.py:279
Async XLA Ops:
  0.6 1.2 %copy-start.1 = (bf16[16,32,1024]{2,1,0:T(8,128)(2,1)S(1)}, bf16[16,32,1024]{2,1,0:T(8,128)(2,1)}, u32[]{:S(2)}) copy-start(bf16[16,32,1024]{2,1,0:T(8,128)(2,1)} %dens_h.1) | copy-start | bytes 3145732
  1.9 0.7 %copy-start.2 = (f32[3,8]{1,0:T(4,128)S(1)}, f32[3,8]{1,0:T(4,128)}, u32[]{:S(2)}) copy-start(f32[3,8]{1,0:T(4,128)} %emit_h.1) | copy-start | bytes 292
  2.5 0.7 %copy-start.3 = (f32[8]{0:T(128)S(1)}, f32[8]{0:T(128)}, u32[]{:S(2)}) copy-start(f32[8]{0:T(128)} %absorb_h.1) | copy-start | bytes 100
  4.0 12.1 %collective-permute-start.2 = (bf16[32,1024]{1,0:T(8,128)(2,1)S(1)}, bf16[32,1024]{1,0:T(8,128)(2,1)S(1)}, u32[]{:S(2)}, u32[]{:S(2)}) collective-permute-start(bf16[32,1024]{1,0:T(8,128)(2,1)S(1)} %get-tuple-element.19), channel_id=1, source_target_pairs={{1,0},{2,1},{3,2},{4,3},{5,4},{6,5},{7,6},{8,7},{9,8},{10,9},{11,1... | collective-permute-start | bytes 196616 | tf_op jit(solution)/shard_map/ppermute | solution.py:252
  6.1 10.0 %collective-permute-start = (bf16[16,1024]{1,0:T(8,128)(2,1)S(1)}, bf16[16,1024]{1,0:T(8,128)(2,1)S(1)}, u32[]{:S(2)}, u32[]{:S(2)}) collective-permute-start(bf16[16,1024]{1,0:T(8,128)(2,1)S(1)} %get-tuple-element.17), channel_id=1, source_target_pairs={{0,32},{32,0},{64,96},{96,64},{128,160},{160,128},{192,224},{224,1... | collective-permute-start | bytes 98312 | tf_op jit(solution)/shard_map/ppermute | solution.py:253
  9.0 7.1 %collective-permute-start.1 = (bf16[16,1024]{1,0:T(8,128)(2,1)S(1)}, bf16[16,1024]{1,0:T(8,128)(2,1)S(1)}, u32[]{:S(2)}, u32[]{:S(2)}) collective-permute-start(bf16[16,1024]{1,0:T(8,128)(2,1)S(1)} %get-tuple-element.18), channel_id=1, source_target_pairs={{32,64},{96,128},{160,192},{224,256},{288,320},{352,384},{416,448}... | collective-permute-start | bytes 98312 | tf_op jit(solution)/shard_map/ppermute | solution.py:254
  12.0 1.6 %copy-start = (s32[16,32,1024]{2,1,0:T(8,128)S(1)}, s32[16,32,1024]{2,1,0:T(8,128)}, u32[]{:S(2)}) copy-start(s32[16,32,1024]{2,1,0:T(8,128)} %mats_h.1) | copy-start | bytes 6291460

commit v3 on v2

--- a/solution.py
+++ b/solution.py
@@ -36,10 +36,12 @@
     return table
 
 
-def edge_kernel(dens_h, emit_h, absorb_h, dens, layer, near, far, tables, edges, emit, absorb, sems):
+def edge_kernel(dens_h, mats_h, emit_h, absorb_h, dens, strip, layer, near, far, tables, edges, emit, absorb, sems):
     cells, rows, cols = dens.shape
     load = pltpu.make_async_copy(dens_h, dens, sems.at[0])
     load.start()
+    load_mats = pltpu.make_async_copy(mats_h.at[:, pl.ds(0, 8), :], strip, sems.at[3])
+    load_mats.start()
     load_emit = pltpu.make_async_copy(emit_h, emit, sems.at[1])
     load_emit.start()
     load_absorb = pltpu.make_async_copy(absorb_h, absorb, sems.at[2])
@@ -58,15 +60,16 @@
     first, last = edges[0], edges[1]
     near[...] = jnp.where(odd == 1, first, last).astype(jnp.bfloat16)
     far[...] = jnp.where(odd == 1, last, first).astype(jnp.bfloat16)
-
-
-def body_kernel(dens, mats_h, tables, sums, final, border, mats, field, sems):
+    load_mats.wait()
+
+
+def body_kernel(dens, strip, mats_h, tables, sums, final, border, mats, field, sems):
     cells, rows, cols = dens.shape
     tiles, strips = cols // 128, rows // 8
     loads = []
-    for r in range(strips):
+    for r in range(1, strips):
         part = pl.ds(8 * r, 8)
-        loads.append(pltpu.make_async_copy(mats_h.at[:, part, :], mats.at[:, part, :], sems.at[r]))
+        loads.append(pltpu.make_async_copy(mats_h.at[:, part, :], mats.at[:, part, :], sems.at[r - 1]))
         loads[-1].start()
     table = [tables[q] for q in range(4)]
     lane = lax.broadcasted_iota(jnp.int32, (8, 128), 1)
@@ -83,6 +86,10 @@
         start = (8 * half * tiles + j) * PITCH + 8 + row_number
         return field[pl.ds(start, 8, stride=tiles * PITCH), :]
 
+    def pick(k, at, count, j):
+        source = strip if at < 8 else mats
+        return source[k, pl.ds(at, count), 128 * j : 128 * (j + 1)]
+
     zero = jnp.zeros((8, 128), jnp.float32)
 
     def across(before, f, behind):
@@ -91,7 +98,8 @@
         return right - left
 
     for r in range(strips):
-        loads[r].wait()
+        if r:
+            loads[r - 1].wait()
         at = 8 * r
         for j0 in range(0, tiles, HALF):
             js = range(j0, j0 + HALF)
@@ -111,7 +119,7 @@
                     if r == strips - 1:
                         lower = jnp.where(row == 7, 0.0, lower)
                     shade = 1.5 + jnp.tanh((lower - upper) + across(wide[n], f, wide[n + 2]))
-                    index = mats[k, pl.ds(at, 8), 128 * j : 128 * (j + 1)]
+                    index = pick(k, at, 8, j)
                     found = [lookup(t, index) for t in table]
                     spot = pl.ds((r * tiles + j) * 8, 8)
                     if last:
@@ -142,7 +150,7 @@
                 nxt = pltpu.roll(f[h][j], 7, 0)
                 twice = f[h][j] + jnp.where(row == 7, behind_first, nxt)
                 index = jnp.concatenate(
-                    [mats[8 * h + i, own : own + 1, 128 * j : 128 * (j + 1)] for i in range(8)], 0
+                    [pick(8 * h + i, own, 1, j) for i in range(8)], 0
                 )
                 found = [lookup(t, index) for t in table]
                 thick = found[0] * twice * twice
@@ -228,27 +236,32 @@
     vmem = pl.BlockSpec(memory_space=pltpu.VMEM)
     smem = pl.BlockSpec(memory_space=pltpu.SMEM)
     hbm = pl.BlockSpec(memory_space=pltpu.HBM)
+    density, materials, emit_table, absorb_table = (
+        pltpu.with_memory_space_constraint(x, pltpu.HBM)
+        for x in (density, materials, emit_table, absorb_table)
+    )
     room = pltpu.CompilerParams(vmem_limit_bytes=32 << 20)
     spots = rows * cols // 128
-    dens, layer, near, far, tables = pl.pallas_call(
+    dens, strip, layer, near, far, tables = pl.pallas_call(
         edge_kernel,
         out_shape=(
             jax.ShapeDtypeStruct(density.shape, density.dtype),
+            jax.ShapeDtypeStruct((cells, 8, cols), materials.dtype),
             jax.ShapeDtypeStruct((rows, cols), density.dtype),
             jax.ShapeDtypeStruct((cells, cols), density.dtype),
             jax.ShapeDtypeStruct((cells, cols), density.dtype),
             jax.ShapeDtypeStruct((4, 8, 128), jnp.float32),
         ),
-        in_specs=[hbm] * 3,
-        out_specs=(vmem,) * 5,
+        in_specs=[hbm] * 4,
+        out_specs=(vmem,) * 6,
         scratch_shapes=[
             pltpu.VMEM((2, cells, cols), jnp.float32),
             pltpu.SMEM(emit_table.shape, jnp.float32),
             pltpu.SMEM(absorb_table.shape, jnp.float32),
-            pltpu.SemaphoreType.DMA((3,)),
+            pltpu.SemaphoreType.DMA((4,)),
         ],
         compiler_params=room,
-    )(density, emit_table, absorb_table)
+    )(density, materials, emit_table, absorb_table)
     after = lax.ppermute(layer, "depth", nearer)
     near = lax.ppermute(near, "tile", swap)
     far = lax.ppermute(far, "tile", cross)
@@ -259,15 +272,15 @@
             jax.ShapeDtypeStruct((6, spots, 128), jnp.float32),
             jax.ShapeDtypeStruct((2, 5, cells, cols), jnp.float32),
         ),
-        in_specs=[vmem, hbm, vmem],
+        in_specs=[vmem, vmem, hbm, vmem],
         out_specs=(vmem,) * 3,
         scratch_shapes=[
             pltpu.VMEM(materials.shape, materials.dtype),
             pltpu.VMEM((cells * (cols // 128) * PITCH, 128), jnp.float32),
-            pltpu.SemaphoreType.DMA((rows // 8,)),
+            pltpu.SemaphoreType.DMA((rows // 8 - 1,)),
         ],
         compiler_params=room,
-    )(dens, materials, tables)
+    )(dens, strip, materials, tables)
     parts = pl.pallas_call(
         join_kernel,
         out_shape=jax.ShapeDtypeStruct((rows, 32, 128), jnp.bfloat16),
@@ -276,6 +289,7 @@
         compiler_params=room,
     )(sums, final, border, near, far, after)
     parts = lax.all_to_all(parts, "depth", 0, 0, tiled=True)
+    parts = pltpu.with_memory_space_constraint(parts, pltpu.VMEM)
     colour, opacity = pl.pallas_call(
         final_kernel,
         out_shape=(

time: 41.1 us -> 37.5 us (0.912)
  the two profiles are of different devices: /device:TPU:265 before, /device:TPU:201 now
where the time goes in v3:
time: 37.5 us; the launch traced here: 37.2 us
  blocking collectives  20.4 us (54%)
  starting transfers between devices  10.1 us (27%)
  Pallas kernels  6.06 us (16%)
  between operations  0.7 us (2%)
    all_to_all x1, blocking collectives, shards(): parts = lax.all_to_all(parts, 'depth', 0, 0, tiled=True)  20.4 us
    ppermute x1, starting transfers between devices, shards(): far = lax.ppermute(far, 'tile', cross)  5.11 us
    ppermute x1, starting transfers between devices, shards(): near = lax.ppermute(near, 'tile', swap)  2.86 us
    pallas_call x1, Pallas kernels, shards(): pl.pallas_call(body_kernel, out_shape=(jax.ShapeDtypeStruct((4, spots, 12...  2.79 us
    ppermute x1, starting transfers between devices, shards(): after = lax.ppermute(layer, 'depth', nearer)  2.08 us
    pallas_call x1, Pallas kernels, shards(): pl.pallas_call(final_kernel, out_shape=(jax.ShapeDtypeStruct((3, 8, 128),...  1.43 us
    pallas_call x1, Pallas kernels, shards(): pl.pallas_call(edge_kernel, out_shape=(jax.ShapeDtypeStruct(density.shape...  1.39 us
  transfers between devices with their start and end apart: 3, of which 0 were waited for; matrix products, arithmetic and copies ran while one was open for 0% of the time, Pallas kernels for 7%

profile of v3, /device:TPU:201, one launch (start us, length us, event | category | flops | bytes accessed | tf_op | source)
XLA Modules:
  0.0 37.2 jit_solution(2695931463071796655)
XLA Ops:
  0.6 1.4 %shard_map.68 = (bf16[16,32,1024]{2,1,0:T(8,128)(2,1)S(1)}, s32[16,8,1024]{2,1,0:T(8,128)S(1)}, bf16[32,1024]{1,0:T(8,128)(2,1)S(1)}, bf16[16,1024]{1,0:T(8,128)...) custom-call(bf16[16,32,1024]{2,1,0:T(8,128)(2,1)} %dens_h.1, s32[16,32,1024]{2,1,0:T(8,128)} %mats_h.3, ...), custom_call_target="tpu_custom_call" | custom-call | tf_op jit(solution)/shard_map/pallas_call | solution.py:245
  2.0 2.1 %collective-permute-start.2 = (bf16[32,1024]{1,0:T(8,128)(2,1)S(1)}, bf16[32,1024]{1,0:T(8,128)(2,1)S(1)}, u32[]{:S(2)}, u32[]{:S(2)}) collective-permute-start(bf16[32,1024]{1,0:T(8,128)(2,1)S(1)} %get-tuple-element.21), channel_id=1, source_target_pairs={{1,0},{2,1},{3,2},{4,3},{5,4},{6,5},{7,6},{8,7},{9,8},{10,9},{11,1... | collective-permute-start | bytes 196616 | tf_op jit(solution)/shard_map/ppermute | solution.py:265
  4.1 2.9 %collective-permute-start = (bf16[16,1024]{1,0:T(8,128)(2,1)S(1)}, bf16[16,1024]{1,0:T(8,128)(2,1)S(1)}, u32[]{:S(2)}, u32[]{:S(2)}) collective-permute-start(bf16[16,1024]{1,0:T(8,128)(2,1)S(1)} %get-tuple-element.19), channel_id=1, source_target_pairs={{0,32},{32,0},{64,96},{96,64},{128,160},{160,128},{192,224},{224,1... | collective-permute-start | bytes 98312 | tf_op jit(solution)/shard_map/ppermute | solution.py:266
  7.0 5.1 %collective-permute-start.1 = (bf16[16,1024]{1,0:T(8,128)(2,1)S(1)}, bf16[16,1024]{1,0:T(8,128)(2,1)S(1)}, u32[]{:S(2)}, u32[]{:S(2)}) collective-permute-start(bf16[16,1024]{1,0:T(8,128)(2,1)S(1)} %get-tuple-element.20), channel_id=1, source_target_pairs={{32,64},{96,128},{160,192},{224,256},{288,320},{352,384},{416,448}... | collective-permute-start | bytes 98312 | tf_op jit(solution)/shard_map/ppermute | solution.py:267
  12.1 2.8 %shard_map.69 = (f32[4,256,128]{2,1,0:T(8,128)S(1)}, f32[6,256,128]{2,1,0:T(8,128)S(1)}, f32[2,5,16,1024]{3,2,1,0:T(8,128)S(1)}) custom-call(bf16[16,32,1024]{2,1,0:T(8,128)(2,1)S(1)} %get-tuple-element.13.dens, s32[16,8,1024]{2,1,0:T(8,128)S(1)} %get-tuple-element.14.strip, s32[16,32,1024]{2,1,0:T(8,128)} %mats_h.3, f32[4,8,128]{2,1,0:T(8,128)S(1)} %get-tuple-element.15.tables), custom_call_target="tpu_custom_call" | custom-call | tf_op jit(solution)/shard_map/pallas_call | solution.py:268
  14.9 0.0 collective-permute-done.near
  14.9 0.0 collective-permute-done.1.far
  14.9 0.0 collective-permute-done.2.after
  14.9 0.4 %shard_map.70 = bf16[32,32,128]{2,1,0:T(8,128)(2,1)S(1)} custom-call(f32[4,256,128]{2,1,0:T(8,128)S(1)} %get-tuple-element.16.sums, f32[6,256,128]{2,1,0:T(8,128)S(1)} %get-tuple-element.17.final, f32[2,5,16,1024]{3,2,1,0:T(8,128)S(1)} %get-tuple-element.18.border, bf16[16,1024]{1,0:T(8,128)(2,1)S(1)} %collective-permute-done.near, ...), custom_call_target="tpu_custom_call" | custom-call | tf_op jit(solution)/shard_map/pallas_call | solution.py:284
  15.4 20.4 %all_to_all.5.parts = bf16[32,32,128]{2,1,0:T(8,128)(2,1)S(1)} all-to-all(bf16[32,32,128]{2,1,0:T(8,128)(2,1)S(1)} %shard_map.70), channel_id=1, replica_groups=mesh['tile'=16,'depth'=32] {'depth'}, dimensions={0} | all-to-all | bytes 524288 | tf_op jit(solution)/shard_map/all_to_all | solution.py:291
  35.8 1.4 %shard_map.71 = (f32[3,8,128]{2,1,0:T(8,128)}, f32[8,128]{1,0:T(8,128)}) custom-call(s32[32]{0:T(128)} %order.1, bf16[32,32,128]{2,1,0:T(8,128)(2,1)S(1)} %all_to_all.5.parts), custom_call_target="tpu_custom_call" | custom-call | tf_op jit(solution)/shard_map/pallas_call | solution.py:293
Async XLA Ops:
  2.0 12.9 %collective-permute-start.2 = (bf16[32,1024]{1,0:T(8,128)(2,1)S(1)}, bf16[32,1024]{1,0:T(8,128)(2,1)S(1)}, u32[]{:S(2)}, u32[]{:S(2)}) collective-permute-start(bf16[32,1024]{1,0:T(8,128)(2,1)S(1)} %get-tuple-element.21), channel_id=1, source_target_pairs={{1,0},{2,1},{3,2},{4,3},{5,4},{6,5},{7,6},{8,7},{9,8},{10,9},{11,1... | collective-permute-start | bytes 196616 | tf_op jit(solution)/shard_map/ppermute | solution.py:265
  4.1 10.8 %collective-permute-start = (bf16[16,1024]{1,0:T(8,128)(2,1)S(1)}, bf16[16,1024]{1,0:T(8,128)(2,1)S(1)}, u32[]{:S(2)}, u32[]{:S(2)}) collective-permute-start(bf16[16,1024]{1,0:T(8,128)(2,1)S(1)} %get-tuple-element.19), channel_id=1, source_target_pairs={{0,32},{32,0},{64,96},{96,64},{128,160},{160,128},{192,224},{224,1... | collective-permute-start | bytes 98312 | tf_op jit(solution)/shard_map/ppermute | solution.py:266
  7.0 7.9 %collective-permute-start.1 = (bf16[16,1024]{1,0:T(8,128)(2,1)S(1)}, bf16[16,1024]{1,0:T(8,128)(2,1)S(1)}, u32[]{:S(2)}, u32[]{:S(2)}) collective-permute-start(bf16[16,1024]{1,0:T(8,128)(2,1)S(1)} %get-tuple-element.20), channel_id=1, source_target_pairs={{32,64},{96,128},{160,192},{224,256},{288,320},{352,384},{416,448}... | collective-permute-start | bytes 98312 | tf_op jit(solution)/shard_map/ppermute | solution.py:267

commit v4 on v3

--- a/solution.py
+++ b/solution.py
@@ -25,7 +25,19 @@
 
 
 def lookup(table, index):
-    return jnp.take_along_axis(table, index, axis=0, mode="promise_in_bounds")
+    return lax.gather(
+        table,
+        index[..., None],
+        lax.GatherDimensionNumbers(
+            offset_dims=(),
+            collapsed_slice_dims=(0,),
+            start_index_map=(0,),
+            operand_batching_dims=(1,),
+            start_indices_batching_dims=(1,),
+        ),
+        slice_sizes=(1, 1),
+        mode=lax.GatherScatterMode.PROMISE_IN_BOUNDS,
+    )
 
 
 def row_table(read):
@@ -97,7 +109,37 @@
         right = pltpu.roll(jnp.where(lane == 0, behind, f), 127, 1)
         return right - left
 
+    def edge(e):
+        own, inner, sign = ((0, 1, 1.0), (rows - 1, rows - 2, -1.0))[e]
+        f = [[along(own, h, j) for j in range(tiles)] for h in range(2)]
+        for j in range(tiles):
+            carried = jnp.zeros((1, 128), jnp.float32)
+            for h in range(2):
+                before = f[h][j - 1] if j else zero
+                behind = f[h][j + 1] if j + 1 < tiles else zero
+                grad = sign * along(inner, h, j) + across(before, f[h][j], behind)
+                behind_first = f[1][j][0:1] if h == 0 else jnp.zeros((1, 128), jnp.float32)
+                nxt = pltpu.roll(f[h][j], 7, 0)
+                twice = f[h][j] + jnp.where(row == 7, behind_first, nxt)
+                index = jnp.concatenate(
+                    [pick(8 * h + i, own, 1, j) for i in range(8)], 0
+                )
+                found = [lookup(t, index) for t in table]
+                thick = found[0] * twice * twice
+                total = thick
+                for step in (1, 2, 4):
+                    total = total + jnp.where(row >= step, pltpu.roll(total, step, 0), 0.0)
+                through = jnp.exp2(total - thick + carried)
+                carried = carried + total[7:8]
+                spot = (pl.ds(8 * h, 8), pl.ds(128 * j, 128))
+                border[e, 0, *spot] = grad
+                border[e, 1, *spot] = twice
+                for c in range(3):
+                    border[e, 2 + c, *spot] = found[1 + c] * through
+
     for r in range(strips):
+        if r == 1:
+            edge(0)
         if r:
             loads[r - 1].wait()
         at = 8 * r
@@ -136,34 +178,7 @@
                     green[n] = green[n] + found[2] * weight
                     blue[n] = blue[n] + found[3] * weight
                 here = nxt
-
-    for e, (own, inner) in enumerate(((0, 1), (rows - 1, rows - 2))):
-        sign = 1.0 if e == 0 else -1.0
-        f = [[along(own, h, j) for j in range(tiles)] for h in range(2)]
-        for j in range(tiles):
-            carried = jnp.zeros((1, 128), jnp.float32)
-            for h in range(2):
-                before = f[h][j - 1] if j else zero
-                behind = f[h][j + 1] if j + 1 < tiles else zero
-                grad = sign * along(inner, h, j) + across(before, f[h][j], behind)
-                behind_first = f[1][j][0:1] if h == 0 else jnp.zeros((1, 128), jnp.float32)
-                nxt = pltpu.roll(f[h][j], 7, 0)
-                twice = f[h][j] + jnp.where(row == 7, behind_first, nxt)
-                index = jnp.concatenate(
-                    [pick(8 * h + i, own, 1, j) for i in range(8)], 0
-                )
-                found = [lookup(t, index) for t in table]
-                thick = found[0] * twice * twice
-                total = thick
-                for step in (1, 2, 4):
-                    total = total + jnp.where(row >= step, pltpu.roll(total, step, 0), 0.0)
-                through = jnp.exp2(total - thick + carried)
-                carried = carried + total[7:8]
-                spot = (pl.ds(8 * h, 8), pl.ds(128 * j, 128))
-                border[e, 0, *spot] = grad
-                border[e, 1, *spot] = twice
-                for c in range(3):
-                    border[e, 2 + c, *spot] = found[1 + c] * through
+    edge(1)
 
 
 def join_kernel(sums, final, border, near, far, after, out):
@@ -210,20 +225,27 @@
         out[pl.ds(8 * r, 8)] = strip.reshape(8, 32, 128)
 
 
-def final_kernel(order, parts, colour, opacity):
+def final_kernel(order, parts, colour_h, opacity_h, colour, opacity, sems):
     slabs = parts.shape[0]
-    front = jnp.zeros((8, 128), jnp.float32)
+    fronts = [jnp.zeros((8, 128), jnp.float32)]
+    for rank in range(slabs):
+        value = parts[order[rank], 16:32, :].astype(jnp.float32)[8:16]
+        fronts.append(fronts[-1] + root16(value) * (-LOG2E / THICK_GAIN))
+    opacity[...] = 1.0 - jnp.exp2(fronts[-1])
+    send_opacity = pltpu.make_async_copy(opacity, opacity_h, sems.at[0])
+    send_opacity.start()
     totals = [jnp.zeros((8, 128), jnp.float32) for _ in range(3)]
     for rank in range(slabs):
-        slab = order[rank]
-        value = root16(parts[slab].astype(jnp.float32))
-        through = jnp.exp2(-front)
+        through = jnp.exp2(fronts[rank]) * (1.0 / IMAGE_GAIN)
+        value = parts[order[rank]].astype(jnp.float32)
         for c in range(3):
-            totals[c] = totals[c] + value[8 * c : 8 * c + 8] * through
-        front = front + value[24:32] * (LOG2E / THICK_GAIN)
+            totals[c] = totals[c] + root16(value[8 * c : 8 * c + 8]) * through
     for c in range(3):
-        colour[c] = totals[c] * (1.0 / IMAGE_GAIN)
-    opacity[...] = 1.0 - jnp.exp2(-front)
+        colour[c] = totals[c]
+    send_colour = pltpu.make_async_copy(colour, colour_h, sems.at[1])
+    send_colour.start()
+    send_opacity.wait()
+    send_colour.wait()
 
 
 def shards(density, materials, emit_table, absorb_table, depth_order):
@@ -276,7 +298,7 @@
         out_specs=(vmem,) * 3,
         scratch_shapes=[
             pltpu.VMEM(materials.shape, materials.dtype),
-            pltpu.VMEM((cells * (cols // 128) * PITCH, 128), jnp.float32),
+            pltpu.VMEM(((cells + 1) * (cols // 128) * PITCH, 128), jnp.float32),
             pltpu.SemaphoreType.DMA((rows // 8 - 1,)),
         ],
         compiler_params=room,
@@ -297,7 +319,12 @@
             jax.ShapeDtypeStruct((8, 128), jnp.float32),
         ),
         in_specs=[smem, vmem],
-        out_specs=(vmem, vmem),
+        out_specs=(hbm, hbm),
+        scratch_shapes=[
+            pltpu.VMEM((3, 8, 128), jnp.float32),
+            pltpu.VMEM((8, 128), jnp.float32),
+            pltpu.SemaphoreType.DMA((2,)),
+        ],
     )(depth_order, parts)
     return colour.reshape(3, 1, cols), opacity.reshape(1, cols)
 

time: 37.5 us -> 37.5 us (level)
  no operation moved by 1% of the time
where the time goes in v4:
time: 37.5 us; the launch traced here: 37.2 us
  blocking collectives  20.6 us (55%)
  starting transfers between devices  10 us (27%)
  Pallas kernels  5.83 us (16%)
  between operations  0.7 us (2%)
    all_to_all x1, blocking collectives, shards(): parts = lax.all_to_all(parts, 'depth', 0, 0, tiled=True)  20.6 us
    ppermute x1, starting transfers between devices, shards(): far = lax.ppermute(far, 'tile', cross)  5.11 us
    ppermute x1, starting transfers between devices, shards(): near = lax.ppermute(near, 'tile', swap)  2.86 us
    pallas_call x1, Pallas kernels, shards(): pl.pallas_call(body_kernel, out_shape=(jax.ShapeDtypeStruct((4, spots, 12...  2.55 us
    ppermute x1, starting transfers between devices, shards(): after = lax.ppermute(layer, 'depth', nearer)  2.08 us
    pallas_call x1, Pallas kernels, shards(): pl.pallas_call(final_kernel, out_shape=(jax.ShapeDtypeStruct((3, 8, 128),...  1.45 us
    pallas_call x1, Pallas kernels, shards(): pl.pallas_call(edge_kernel, out_shape=(jax.ShapeDtypeStruct(density.shape...  1.39 us
  transfers between devices with their start and end apart: 3, of which 0 were waited for; matrix products, arithmetic and copies ran while one was open for 0% of the time, Pallas kernels for 7%

profile of v4, /device:TPU:201, one launch (start us, length us, event | category | flops | bytes accessed | tf_op | source)
XLA Modules:
  0.0 37.2 jit_solution(3700780512606794320)
XLA Ops:
  0.6 1.4 %shard_map.68 = (bf16[16,32,1024]{2,1,0:T(8,128)(2,1)S(1)}, s32[16,8,1024]{2,1,0:T(8,128)S(1)}, bf16[32,1024]{1,0:T(8,128)(2,1)S(1)}, bf16[16,1024]{1,0:T(8,128)...) custom-call(bf16[16,32,1024]{2,1,0:T(8,128)(2,1)} %dens_h.1, s32[16,32,1024]{2,1,0:T(8,128)} %mats_h.3, ...), custom_call_target="tpu_custom_call" | custom-call | tf_op jit(solution)/shard_map/pallas_call | solution.py:267
  2.0 2.1 %collective-permute-start.2 = (bf16[32,1024]{1,0:T(8,128)(2,1)S(1)}, bf16[32,1024]{1,0:T(8,128)(2,1)S(1)}, u32[]{:S(2)}, u32[]{:S(2)}) collective-permute-start(bf16[32,1024]{1,0:T(8,128)(2,1)S(1)} %get-tuple-element.21), channel_id=1, source_target_pairs={{1,0},{2,1},{3,2},{4,3},{5,4},{6,5},{7,6},{8,7},{9,8},{10,9},{11,1... | collective-permute-start | bytes 196616 | tf_op jit(solution)/shard_map/ppermute | solution.py:287
  4.1 2.9 %collective-permute-start = (bf16[16,1024]{1,0:T(8,128)(2,1)S(1)}, bf16[16,1024]{1,0:T(8,128)(2,1)S(1)}, u32[]{:S(2)}, u32[]{:S(2)}) collective-permute-start(bf16[16,1024]{1,0:T(8,128)(2,1)S(1)} %get-tuple-element.19), channel_id=1, source_target_pairs={{0,32},{32,0},{64,96},{96,64},{128,160},{160,128},{192,224},{224,1... | collective-permute-start | bytes 98312 | tf_op jit(solution)/shard_map/ppermute | solution.py:288
  7.0 5.1 %collective-permute-start.1 = (bf16[16,1024]{1,0:T(8,128)(2,1)S(1)}, bf16[16,1024]{1,0:T(8,128)(2,1)S(1)}, u32[]{:S(2)}, u32[]{:S(2)}) collective-permute-start(bf16[16,1024]{1,0:T(8,128)(2,1)S(1)} %get-tuple-element.20), channel_id=1, source_target_pairs={{32,64},{96,128},{160,192},{224,256},{288,320},{352,384},{416,448}... | collective-permute-start | bytes 98312 | tf_op jit(solution)/shard_map/ppermute | solution.py:289
  12.1 2.5 %shard_map.69 = (f32[4,256,128]{2,1,0:T(8,128)S(1)}, f32[6,256,128]{2,1,0:T(8,128)S(1)}, f32[2,5,16,1024]{3,2,1,0:T(8,128)S(1)}) custom-call(bf16[16,32,1024]{2,1,0:T(8,128)(2,1)S(1)} %get-tuple-element.13.dens, s32[16,8,1024]{2,1,0:T(8,128)S(1)} %get-tuple-element.14.strip, s32[16,32,1024]{2,1,0:T(8,128)} %mats_h.3, f32[4,8,128]{2,1,0:T(8,128)S(1)} %get-tuple-element.15.tables), custom_call_target="tpu_custom_call" | custom-call | tf_op jit(solution)/shard_map/pallas_call | solution.py:290
  14.7 0.0 collective-permute-done.near
  14.7 0.0 collective-permute-done.1.far
  14.7 0.0 collective-permute-done.2.after
  14.7 0.4 %shard_map.70 = bf16[32,32,128]{2,1,0:T(8,128)(2,1)S(1)} custom-call(f32[4,256,128]{2,1,0:T(8,128)S(1)} %get-tuple-element.16.sums, f32[6,256,128]{2,1,0:T(8,128)S(1)} %get-tuple-element.17.final, f32[2,5,16,1024]{3,2,1,0:T(8,128)S(1)} %get-tuple-element.18.border, bf16[16,1024]{1,0:T(8,128)(2,1)S(1)} %collective-permute-done.near, ...), custom_call_target="tpu_custom_call" | custom-call | tf_op jit(solution)/shard_map/pallas_call | solution.py:306
  15.1 20.6 %all_to_all.5.parts = bf16[32,32,128]{2,1,0:T(8,128)(2,1)S(1)} all-to-all(bf16[32,32,128]{2,1,0:T(8,128)(2,1)S(1)} %shard_map.70), channel_id=1, replica_groups=mesh['tile'=16,'depth'=32] {'depth'}, dimensions={0} | all-to-all | bytes 524288 | tf_op jit(solution)/shard_map/all_to_all | solution.py:313
  35.8 1.4 %shard_map.71 = (f32[3,8,128]{2,1,0:T(8,128)}, f32[8,128]{1,0:T(8,128)}) custom-call(s32[32]{0:T(128)} %order.1, bf16[32,32,128]{2,1,0:T(8,128)(2,1)S(1)} %all_to_all.5.parts), custom_call_target="tpu_custom_call" | custom-call | tf_op jit(solution)/shard_map/pallas_call | solution.py:315
Async XLA Ops:
  2.0 12.7 %collective-permute-start.2 = (bf16[32,1024]{1,0:T(8,128)(2,1)S(1)}, bf16[32,1024]{1,0:T(8,128)(2,1)S(1)}, u32[]{:S(2)}, u32[]{:S(2)}) collective-permute-start(bf16[32,1024]{1,0:T(8,128)(2,1)S(1)} %get-tuple-element.21), channel_id=1, source_target_pairs={{1,0},{2,1},{3,2},{4,3},{5,4},{6,5},{7,6},{8,7},{9,8},{10,9},{11,1... | collective-permute-start | bytes 196616 | tf_op jit(solution)/shard_map/ppermute | solution.py:287
  4.1 10.5 %collective-permute-start = (bf16[16,1024]{1,0:T(8,128)(2,1)S(1)}, bf16[16,1024]{1,0:T(8,128)(2,1)S(1)}, u32[]{:S(2)}, u32[]{:S(2)}) collective-permute-start(bf16[16,1024]{1,0:T(8,128)(2,1)S(1)} %get-tuple-element.19), channel_id=1, source_target_pairs={{0,32},{32,0},{64,96},{96,64},{128,160},{160,128},{192,224},{224,1... | collective-permute-start | bytes 98312 | tf_op jit(solution)/shard_map/ppermute | solution.py:288
  7.0 7.7 %collective-permute-start.1 = (bf16[16,1024]{1,0:T(8,128)(2,1)S(1)}, bf16[16,1024]{1,0:T(8,128)(2,1)S(1)}, u32[]{:S(2)}, u32[]{:S(2)}) collective-permute-start(bf16[16,1024]{1,0:T(8,128)(2,1)S(1)} %get-tuple-element.20), channel_id=1, source_target_pairs={{32,64},{96,128},{160,192},{224,256},{288,320},{352,384},{416,448}... | collective-permute-start | bytes 98312 | tf_op jit(solution)/shard_map/ppermute | solution.py:289

commit v5 on v4

--- a/solution.py
+++ b/solution.py
@@ -48,7 +48,7 @@
     return table
 
 
-def edge_kernel(dens_h, mats_h, emit_h, absorb_h, dens, strip, layer, near, far, tables, edges, emit, absorb, sems):
+def edge_kernel(dens_h, mats_h, emit_h, absorb_h, dens, strip, layer, near, far, tables, turn, edges, emit, absorb, sems):
     cells, rows, cols = dens.shape
     load = pltpu.make_async_copy(dens_h, dens, sems.at[0])
     load.start()
@@ -58,6 +58,9 @@
     load_emit.start()
     load_absorb = pltpu.make_async_copy(absorb_h, absorb, sems.at[2])
     load_absorb.start()
+    a = lax.broadcasted_iota(jnp.int32, (256, 256), 0)
+    b = lax.broadcasted_iota(jnp.int32, (256, 256), 1)
+    turn[...] = jnp.where((a // 32 == b % 8) & (a % 32 == b // 8), 1.0, 0.0).astype(jnp.bfloat16)
     load_absorb.wait()
     load_emit.wait()
     tables[0] = row_table(lambda m: absorb[m] * (-0.25 * LOG2E))
@@ -70,7 +73,7 @@
         edges[1, pl.ds(k, 1), :] = dens[k, rows - 1 : rows, :].astype(jnp.float32)
     odd = lax.axis_index("tile") % 2
     first, last = edges[0], edges[1]
-    near[...] = jnp.where(odd == 1, first, last).astype(jnp.bfloat16)
+    near[...] = jnp.where(odd == 1, first, last)
     far[...] = jnp.where(odd == 1, last, first).astype(jnp.bfloat16)
     load_mats.wait()
 
@@ -181,7 +184,7 @@
     edge(1)
 
 
-def join_kernel(sums, final, border, near, far, after, out):
+def join_kernel(sums, final, border, near, after, far, turn, out):
     cells, cols = near.shape
     rows = after.shape[0]
     tiles, strips = cols // 128, rows // 8
@@ -198,9 +201,6 @@
         twice = border[e, 1] + jnp.where(cell == cells - 1, own, 0.0)
         weight = twice * (1.5 + jnp.tanh(border[e, 0] + halo))
         outer.append([jnp.sum(border[e, 2 + c] * weight, 0, keepdims=True) for c in range(3)])
-    a = lax.broadcasted_iota(jnp.int32, (256, 256), 0)
-    b = lax.broadcasted_iota(jnp.int32, (256, 256), 1)
-    turn = jnp.where((a // 32 == b % 8) & (a % 32 == b // 8), 1.0, 0.0).astype(jnp.bfloat16)
     stacks = []
     for r in range(strips):
         block = [[None] * tiles for _ in range(4)]
@@ -219,7 +219,7 @@
                 block[c][j] = power16(value)
             block[3][j] = power16(inside * (-THICK_GAIN / LOG2E))
         stacks.append(jnp.concatenate([v for c in block for v in c], 0).astype(jnp.bfloat16))
-    moved = jnp.dot(turn, jnp.concatenate(stacks, 1), preferred_element_type=jnp.float32)
+    moved = jnp.dot(turn[...], jnp.concatenate(stacks, 1), preferred_element_type=jnp.float32)
     for r in range(strips):
         strip = moved[:, 128 * r : 128 * (r + 1)].astype(jnp.bfloat16)
         out[pl.ds(8 * r, 8)] = strip.reshape(8, 32, 128)
@@ -264,18 +264,19 @@
     )
     room = pltpu.CompilerParams(vmem_limit_bytes=32 << 20)
     spots = rows * cols // 128
-    dens, strip, layer, near, far, tables = pl.pallas_call(
+    dens, strip, layer, near, far, tables, turn = pl.pallas_call(
         edge_kernel,
         out_shape=(
             jax.ShapeDtypeStruct(density.shape, density.dtype),
             jax.ShapeDtypeStruct((cells, 8, cols), materials.dtype),
             jax.ShapeDtypeStruct((rows, cols), density.dtype),
-            jax.ShapeDtypeStruct((cells, cols), density.dtype),
+            jax.ShapeDtypeStruct((cells, cols), jnp.float32),
             jax.ShapeDtypeStruct((cells, cols), density.dtype),
             jax.ShapeDtypeStruct((4, 8, 128), jnp.float32),
+            jax.ShapeDtypeStruct((256, 256), jnp.bfloat16),
         ),
         in_specs=[hbm] * 4,
-        out_specs=(vmem,) * 6,
+        out_specs=(vmem,) * 7,
         scratch_shapes=[
             pltpu.VMEM((2, cells, cols), jnp.float32),
             pltpu.SMEM(emit_table.shape, jnp.float32),
@@ -306,10 +307,10 @@
     parts = pl.pallas_call(
         join_kernel,
         out_shape=jax.ShapeDtypeStruct((rows, 32, 128), jnp.bfloat16),
-        in_specs=[vmem] * 6,
+        in_specs=[vmem] * 7,
         out_specs=vmem,
         compiler_params=room,
-    )(sums, final, border, near, far, after)
+    )(sums, final, border, near, after, far, turn)
     parts = lax.all_to_all(parts, "depth", 0, 0, tiled=True)
     parts = pltpu.with_memory_space_constraint(parts, pltpu.VMEM)
     colour, opacity = pl.pallas_call(

time: 37.5 us -> 37.5 us (level)
  no operation moved by 1% of the time
where the time goes in v5:
time: 37.5 us; the launch traced here: 37.2 us
  blocking collectives  20.6 us (55%)
  starting transfers between devices  10.1 us (27%)
  Pallas kernels  5.82 us (16%)
  between operations  0.7 us (2%)
    all_to_all x1, blocking collectives, shards(): parts = lax.all_to_all(parts, 'depth', 0, 0, tiled=True)  20.6 us
    ppermute x1, starting transfers between devices, shards(): far = lax.ppermute(far, 'tile', cross)  5.39 us
    ppermute x1, starting transfers between devices, shards(): near = lax.ppermute(near, 'tile', swap)  2.58 us
    pallas_call x1, Pallas kernels, shards(): pl.pallas_call(body_kernel, out_shape=(jax.ShapeDtypeStruct((4, spots, 12...  2.55 us
    ppermute x1, starting transfers between devices, shards(): after = lax.ppermute(layer, 'depth', nearer)  2.08 us
    pallas_call x1, Pallas kernels, shards(): pl.pallas_call(final_kernel, out_shape=(jax.ShapeDtypeStruct((3, 8, 128),...  1.45 us
    pallas_call x1, Pallas kernels, shards(): pl.pallas_call(edge_kernel, out_shape=(jax.ShapeDtypeStruct(density.shape...  1.39 us
  transfers between devices with their start and end apart: 3, of which 0 were waited for; matrix products, arithmetic and copies ran while one was open for 0% of the time, Pallas kernels for 7%

profile of v5, /device:TPU:201, one launch (start us, length us, event | category | flops | bytes accessed | tf_op | source)
XLA Modules:
  0.0 37.2 jit_solution(4753557674916941880)
XLA Ops:
  0.6 1.4 %shard_map.68 = (bf16[16,32,1024]{2,1,0:T(8,128)(2,1)S(1)}, s32[16,8,1024]{2,1,0:T(8,128)S(1)}, bf16[32,1024]{1,0:T(8,128)(2,1)S(1)}, f32[16,1024]{1,0:T(8,128)S...) custom-call(bf16[16,32,1024]{2,1,0:T(8,128)(2,1)} %dens_h.1, ...), custom_call_target="tpu_custom_call" | custom-call | tf_op jit(solution)/shard_map/pallas_call | solution.py:267
  2.0 2.6 %collective-permute-start = (f32[16,1024]{1,0:T(8,128)S(1)}, f32[16,1024]{1,0:T(8,128)S(1)}, u32[]{:S(2)}, u32[]{:S(2)}) collective-permute-start(f32[16,1024]{1,0:T(8,128)S(1)} %get-tuple-element.20), channel_id=1, source_target_pairs={{0,32},{32,0},{64,96},{96,64},{128,160},{160,128},{192,224},{224,1... | collective-permute-start | bytes 196616 | tf_op jit(solution)/shard_map/ppermute | solution.py:289
  4.6 2.1 %collective-permute-start.1 = (bf16[32,1024]{1,0:T(8,128)(2,1)S(1)}, bf16[32,1024]{1,0:T(8,128)(2,1)S(1)}, u32[]{:S(2)}, u32[]{:S(2)}) collective-permute-start(bf16[32,1024]{1,0:T(8,128)(2,1)S(1)} %get-tuple-element.21), channel_id=1, source_target_pairs={{1,0},{2,1},{3,2},{4,3},{5,4},{6,5},{7,6},{8,7},{9,8},{10,9},{11,1... | collective-permute-start | bytes 196616 | tf_op jit(solution)/shard_map/ppermute | solution.py:288
  6.7 5.4 %collective-permute-start.2 = (bf16[16,1024]{1,0:T(8,128)(2,1)S(1)}, bf16[16,1024]{1,0:T(8,128)(2,1)S(1)}, u32[]{:S(2)}, u32[]{:S(2)}) collective-permute-start(bf16[16,1024]{1,0:T(8,128)(2,1)S(1)} %get-tuple-element.22), channel_id=1, source_target_pairs={{32,64},{96,128},{160,192},{224,256},{288,320},{352,384},{416,448}... | collective-permute-start | bytes 98312 | tf_op jit(solution)/shard_map/ppermute | solution.py:290
  12.1 2.5 %shard_map.69 = (f32[4,256,128]{2,1,0:T(8,128)S(1)}, f32[6,256,128]{2,1,0:T(8,128)S(1)}, f32[2,5,16,1024]{3,2,1,0:T(8,128)S(1)}) custom-call(bf16[16,32,1024]{2,1,0:T(8,128)(2,1)S(1)} %get-tuple-element.14.dens, s32[16,8,1024]{2,1,0:T(8,128)S(1)} %get-tuple-element.15.strip, s32[16,32,1024]{2,1,0:T(8,128)} %mats_h.3, f32[4,8,128]{2,1,0:T(8,128)S(1)} %get-tuple-element.16.tables), custom_call_target="tpu_custom_call" | custom-call | tf_op jit(solution)/shard_map/pallas_call | solution.py:291
  14.7 0.0 collective-permute-done.2.far
  14.7 0.0 collective-permute-done.near
  14.7 0.0 collective-permute-done.1.after
  14.7 0.4 %shard_map.70 = bf16[32,32,128]{2,1,0:T(8,128)(2,1)S(1)} custom-call(f32[4,256,128]{2,1,0:T(8,128)S(1)} %get-tuple-element.17.sums, f32[6,256,128]{2,1,0:T(8,128)S(1)} %get-tuple-element.18.final, f32[2,5,16,1024]{3,2,1,0:T(8,128)S(1)} %get-tuple-element.19.border, f32[16,1024]{1,0:T(8,128)S(1)} %collective-permute-done.near, ...), custom_call_target="tpu_custom_call" | custom-call | tf_op jit(solution)/shard_map/pallas_call | solution.py:307
  15.1 20.6 %all_to_all.5.parts = bf16[32,32,128]{2,1,0:T(8,128)(2,1)S(1)} all-to-all(bf16[32,32,128]{2,1,0:T(8,128)(2,1)S(1)} %shard_map.70), channel_id=1, replica_groups=mesh['tile'=16,'depth'=32] {'depth'}, dimensions={0} | all-to-all | bytes 524288 | tf_op jit(solution)/shard_map/all_to_all | solution.py:314
  35.8 1.4 %shard_map.71 = (f32[3,8,128]{2,1,0:T(8,128)}, f32[8,128]{1,0:T(8,128)}) custom-call(s32[32]{0:T(128)} %order.1, bf16[32,32,128]{2,1,0:T(8,128)(2,1)S(1)} %all_to_all.5.parts), custom_call_target="tpu_custom_call" | custom-call | tf_op jit(solution)/shard_map/pallas_call | solution.py:316
Async XLA Ops:
  2.0 12.6 %collective-permute-start = (f32[16,1024]{1,0:T(8,128)S(1)}, f32[16,1024]{1,0:T(8,128)S(1)}, u32[]{:S(2)}, u32[]{:S(2)}) collective-permute-start(f32[16,1024]{1,0:T(8,128)S(1)} %get-tuple-element.20), channel_id=1, source_target_pairs={{0,32},{32,0},{64,96},{96,64},{128,160},{160,128},{192,224},{224,1... | collective-permute-start | bytes 196616 | tf_op jit(solution)/shard_map/ppermute | solution.py:289
  4.6 10.1 %collective-permute-start.1 = (bf16[32,1024]{1,0:T(8,128)(2,1)S(1)}, bf16[32,1024]{1,0:T(8,128)(2,1)S(1)}, u32[]{:S(2)}, u32[]{:S(2)}) collective-permute-start(bf16[32,1024]{1,0:T(8,128)(2,1)S(1)} %get-tuple-element.21), channel_id=1, source_target_pairs={{1,0},{2,1},{3,2},{4,3},{5,4},{6,5},{7,6},{8,7},{9,8},{10,9},{11,1... | collective-permute-start | bytes 196616 | tf_op jit(solution)/shard_map/ppermute | solution.py:288
  6.7 8.0 %collective-permute-start.2 = (bf16[16,1024]{1,0:T(8,128)(2,1)S(1)}, bf16[16,1024]{1,0:T(8,128)(2,1)S(1)}, u32[]{:S(2)}, u32[]{:S(2)}) collective-permute-start(bf16[16,1024]{1,0:T(8,128)(2,1)S(1)} %get-tuple-element.22), channel_id=1, source_target_pairs={{32,64},{96,128},{160,192},{224,256},{288,320},{352,384},{416,448}... | collective-permute-start | bytes 98312 | tf_op jit(solution)/shard_map/ppermute | solution.py:290
